TPU v7x, 32 devices: a whole 2x2x4 slice. The times are simulated.
32 devices in a mesh: subj: 4 (over z), vox: 8 (over y, x, core).
Axes of the slice: x: 2, y: 2, z: 4, core: 2. Of those that a mesh axis runs over, the one named last changes fastest.
Arguments:
- features: bfloat16 [4096, 4096], P(('subj', 'vox')), may hold values from -20 to 20
- token_ticks: int32 [4096], replicated, may hold values from 0 to 24575, as said below
- offsets: int32 [4], P('subj'), may hold values from 0 to 63
- run_lengths: int32 [4, 8], P('subj'), may hold values from 1 to 128, 384 in all within a row
- penalty: float32 [4], P('subj'), may hold values from 0.05 to 0.5
- responses: float32 [4, 384, 1024], P('subj', None, 'vox'), may hold values from -6 to 6
Outputs:
- weights: bfloat16 [4, 4, 4096, 1024], P('subj', None, 'vox')
Inputs may be any that keep to these rules, and one draw needn't show every extreme that they name: `token_ticks`: token k's tick lies between k * 6 and k * 6 + 5. `run_lengths`: each subject's 8 runs together cover its 384 TRs in order.
All inputs are finite; a program needn't handle non-finite values.
Results may differ from a plain program's by a relative error of at most 0.023.
The roundings to bfloat16 on the way count: a program that leaves them out, or rounds other values in their place, can miss the bound.
Values may be sent and summed in bfloat16 or wider, within the bound.
A program may use at most 128 MiB of HBM per device.

v0:
```python
import math

import jax
import jax.numpy as jnp
from jax import lax
from jax.sharding import PartitionSpec as P

DELAYS = 4
TICKS = 64
GAP = 6


def lanczos_block(near_ticks, offset, first_row, row_count):
    tr_rows = first_row + jnp.arange(row_count, dtype=jnp.int32)
    distance = near_ticks[None, :] - (tr_rows[:, None] * TICKS + offset)
    inside = jnp.abs(distance) < 3 * TICKS
    scaled = distance.astype(jnp.float32) / TICKS
    shaped = jnp.sinc(scaled) * jnp.sinc(scaled / 3.0)
    return jnp.where(inside, shaped, jnp.zeros_like(shaped)).astype(jnp.bfloat16)


def delay_stack(interp, lengths, tr_total):
    starts = jnp.cumsum(lengths) - lengths
    tr_steps = jnp.arange(tr_total, dtype=jnp.int32)
    run_first = jnp.max(jnp.where(starts[None, :] <= tr_steps[:, None], starts[None, :], 0), axis=1)
    delayed = []
    for delay_step in range(1, DELAYS + 1):
        moved = jnp.concatenate(
            [jnp.zeros((delay_step, interp.shape[1]), interp.dtype), interp[:-delay_step]], axis=0
        )
        keep_rows = (tr_steps - delay_step >= run_first)[:, None]
        delayed.append(jnp.where(keep_rows, moved, jnp.zeros_like(moved)))
    return jnp.stack(delayed, axis=1)


def body(features, token_ticks, offsets, run_lengths, penalty, responses):
    tok_dev = features.shape[0]
    width = features.shape[1]
    group_count = lax.axis_size("subj")
    vox_count = lax.axis_size("vox")
    slab_width = width // vox_count
    grouped = lax.all_gather(features, "subj", axis=0, tiled=True)
    mixed_rows = lax.all_to_all(grouped, "vox", split_axis=1, concat_axis=0, tiled=True)
    columns = mixed_rows.reshape(vox_count, group_count, tok_dev, slab_width)
    columns = columns.transpose(1, 0, 2, 3).reshape(vox_count * group_count * tok_dev, slab_width)
    token_count = columns.shape[0]
    tr_total = token_count * GAP // TICKS
    row_block = math.gcd(tr_total, 128)
    window = min((row_block + 5) * TICKS // GAP + 3, token_count)
    offset = offsets[0]
    spread = (GAP / TICKS) ** 0.5

    def interp_block(block_index):
        first_row = block_index * row_block
        lowest_tick = first_row * TICKS + offset - 3 * TICKS
        begin_token = jnp.clip((lowest_tick - GAP + 1) // GAP, 0, token_count - window)
        shard_piece = lax.dynamic_slice_in_dim(columns, begin_token, window, 0)
        near_ticks = lax.dynamic_slice_in_dim(token_ticks, begin_token, window, 0)
        weights_table = lanczos_block(near_ticks, offset, first_row, row_block)
        return jnp.dot(weights_table, shard_piece, preferred_element_type=jnp.float32)

    summed = lax.map(interp_block, jnp.arange(tr_total // row_block, dtype=jnp.int32))
    interp = (summed.reshape(tr_total, slab_width) * spread).astype(jnp.bfloat16)
    stacked = delay_stack(interp, run_lengths[0], tr_total).reshape(tr_total, DELAYS * slab_width)
    partial_kernel = lax.dot_general(
        stacked, stacked, (((1,), (1,)), ((), ())), preferred_element_type=jnp.float32
    )
    kernel = lax.psum(partial_kernel, "vox") / (DELAYS * width)
    system = kernel + penalty[0] * jnp.eye(tr_total, dtype=jnp.float32)
    factor = jnp.linalg.cholesky(system)
    forward = lax.linalg.triangular_solve(factor, responses[0], left_side=True, lower=True)
    dual_coef = lax.linalg.triangular_solve(
        factor, forward, left_side=True, lower=True, transpose_a=True
    ).astype(jnp.bfloat16)
    projected = lax.dot_general(
        stacked,
        lax.all_gather(dual_coef, "vox", axis=1, tiled=True),
        (((0,), (0,)), ((), ())),
        preferred_element_type=jnp.float32,
    )
    projected = (projected * (DELAYS * width) ** (-0.5)).astype(jnp.bfloat16)
    return projected.reshape(1, DELAYS, slab_width, projected.shape[1])


def solution(mesh):
    return jax.shard_map(
        body,
        mesh=mesh,
        in_specs=(
            P(("subj", "vox"), None),
            P(),
            P("subj"),
            P("subj", None),
            P("subj"),
            P("subj", None, "vox"),
        ),
        out_specs=P("subj", None, "vox", None),
        check_vma=False,
    )
```

profile of v0, /device:TPU:0, one launch (start us, length us, event | category | flops | bytes accessed | tf_op | source)
XLA Modules:
  0.0 354.9 jit_solution(4294370341584314719)
XLA Ops:
  6.5 2.3 copy.36
  8.8 83.4 %all-gather.2.cloned.1.call-done = bf16[512,4096]{0,1:T(8,128)(2,1)} async-done(((bf16[128,4096]{0,1:T(8,128)(2,1)}), bf16[512,4096]{0,1:T(8,128)(2,1)}) %all-gather.2.cloned.1.call-update) | async-done | bytes 4194320 | tf_op jit(solution)/shard_map/all_gather | solution.py:42
  92.2 4.7 %all-to-all-start = ((bf16[512,8,512]{0,2,1:T(8,128)(2,1)}), bf16[512,8,512]{0,2,1:T(8,128)(2,1)}, u32[]{:S(2)}, u32[]{:S(2)}) async-start(bf16[512,8,512]{0,2,1:T(8,128)(2,1)} %bitcast.106), calls=%async_computation | async-start | bytes 8388608 | tf_op jit(solution)/shard_map/all_to_all | solution.py:43
  97.0 0.2 reduce-window_clone.1
  97.3 48.8 %all-to-all-done = bf16[512,8,512]{0,2,1:T(8,128)(2,1)} async-done(((bf16[512,8,512]{0,2,1:T(8,128)(2,1)}), bf16[512,8,512]{0,2,1:T(8,128)(2,1)}, u32[]{:S(2)}, u32[]{:S(2)}) %all-to-all-start) | async-done | bytes 4194336 | tf_op jit(solution)/shard_map/all_to_all | solution.py:43
  146.0 6.4 %copy.37 = bf16[8,512,512]{2,1,0:T(8,128)(2,1)} copy(bf16[8,512,512]{1,2,0:T(8,128)(2,1)} %bitcast.6) | data formatting | bytes 8388608 | tf_op jit(solution)/shard_map/all_to_all | solution.py:43
  152.5 4.6 %copy.38 = bf16[4,8,128,512]{3,2,1,0:T(8,128)(2,1)} copy(bf16[4,8,128,512]{3,2,0,1:T(8,128)(2,1)} %bitcast.100) | data formatting | bytes 8388608 | tf_op jit(solution)/shard_map/transpose | solution.py:45
  157.1 21.4 %while.15 = (s32[]{:T(128)}, f32[3,128,512]{2,1,0:T(8,128)S(1)}, s32[3]{0:T(128)S(1)}, s32[]{:T(128)}, s32[4096]{0:T(1024)S(1)}, /*index=5*/bf16[4096,512]{1,0:T...) while((s32[]{:T(128)}, f32[3,128,512]{2,1,0:T(8,128)S(1)}, ...), condition=%wide.region_3.5_spmd, body=%wide.region_2.4_spmd.sunk | while | flops 199895312 | bytes 1741727 | solution.py:62
  157.1 0.6 dynamic_slice.38
  159.7 0.7 multiply_add_fusion.4
  160.4 3.8 %fusion.132 = f32[3,128,512]{2,1,0:T(8,128)S(1)} fusion(f32[3,128,512]{2,1,0:T(8,128)S(1)} %get-tuple-element.277, s32[]{:T(128)} %get-tuple-element.276, bf16[4096,512]{1,0:T(8,128)(2,1)} %get-tuple-element.295, s32[]{:T(128)S(6)} %min.11, s32[128]{0:T(128)S(1)} %multiply_add_fusion.4, s32[1421]{0:T(1024)S(1)} %dynamic_slice.39), kind=kOutput, calls=%fused_computation.9.clone.1 | convolution fusion | flops 199894912 | bytes 1729540 | tf_op jit(solution)/shard_map/while/body/eval_jaxpr/dot_general | solution.py:60
  164.2 0.6 dynamic_slice.38
  166.8 0.7 multiply_add_fusion.4
  167.5 3.8 %fusion.132 = f32[3,128,512]{2,1,0:T(8,128)S(1)} fusion(f32[3,128,512]{2,1,0:T(8,128)S(1)} %get-tuple-element.277, s32[]{:T(128)} %get-tuple-element.276, bf16[4096,512]{1,0:T(8,128)(2,1)} %get-tuple-element.295, s32[]{:T(128)S(6)} %min.11, s32[128]{0:T(128)S(1)} %multiply_add_fusion.4, s32[1421]{0:T(1024)S(1)} %dynamic_slice.39), kind=kOutput, calls=%fused_computation.9.clone.1 | convolution fusion | flops 199894912 | bytes 1729540 | tf_op jit(solution)/shard_map/while/body/eval_jaxpr/dot_general | solution.py:60
  171.3 0.6 dynamic_slice.38
  174.0 0.7 multiply_add_fusion.4
  174.6 3.8 %fusion.132 = f32[3,128,512]{2,1,0:T(8,128)S(1)} fusion(f32[3,128,512]{2,1,0:T(8,128)S(1)} %get-tuple-element.277, s32[]{:T(128)} %get-tuple-element.276, bf16[4096,512]{1,0:T(8,128)(2,1)} %get-tuple-element.295, s32[]{:T(128)S(6)} %min.11, s32[128]{0:T(128)S(1)} %multiply_add_fusion.4, s32[1421]{0:T(1024)S(1)} %dynamic_slice.39), kind=kOutput, calls=%fused_computation.9.clone.1 | convolution fusion | flops 199894912 | bytes 1729540 | tf_op jit(solution)/shard_map/while/body/eval_jaxpr/dot_general | solution.py:60
  178.5 0.3 select_bitcast_fusion.2
  178.8 0.3 select_bitcast_fusion
  179.1 0.2 pad_maximum_fusion
  179.3 1.8 convolution_bitcast_fusion
  181.8 1.1 copy.39
  182.8 49.8 %all-reduce.7.cloned.1.call-done = f32[384,384]{0,1:T(8,128)} async-done(((f32[384,384]{0,1:T(8,128)}), f32[384,384]{0,1:T(8,128)}) %all-reduce.7.cloned.1.call-update) | async-done | bytes 589840 | tf_op jit(solution)/shard_map/psum | solution.py:68
  232.6 1.2 select_add_fusion
  233.8 0.2 copy.41
  234.1 0.1 fusion.84
  234.2 11.7 %cholesky.76 = f32[128,128]{1,0:T(8,128)S(1)} custom-call(f32[128,128]{1,0:T(8,128)S(1)} %cholesky.189), custom_call_target="Cholesky" | custom-call | tf_op jit(solution)/shard_map/jit(cholesky)/cholesky | solution.py:70
  245.9 9.8 %custom-call.24 = f32[1,128,128]{1,2,0:T(8,128)S(1)} custom-call(f32[1,128,128]{2,1,0:T(8,128)S(1)} %get-tuple-element.183), custom_call_target="InvertDiagBlocksLowerTriangular" | custom-call | tf_op jit(solution)/shard_map/jit(cholesky)/cholesky | solution.py:70
  255.7 0.3 fusion.88
  256.0 0.3 convolution_subtract_fusion
  256.3 11.7 %cholesky.160 = f32[128,128]{1,0:T(8,128)S(1)} custom-call(f32[128,128]{1,0:T(8,128)S(1)} %cholesky.193), custom_call_target="Cholesky" | custom-call | tf_op jit(solution)/shard_map/jit(cholesky)/cholesky | solution.py:70
  268.0 0.1 copy.44
  268.1 0.1 copy.43
  268.3 10.0 %custom-call.25 = f32[1,128,128]{1,2,0:T(8,128)S(1)} custom-call(f32[1,128,128]{2,1,0:T(8,128)S(1)} %get-tuple-element.181), custom_call_target="InvertDiagBlocksLowerTriangular" | custom-call | tf_op jit(solution)/shard_map/jit(cholesky)/cholesky | solution.py:70
  278.4 0.3 convolution_dynamic-update-slice_fusion
  278.7 0.4 convolution_subtract_fusion.5
  279.1 11.7 %cholesky.179 = f32[128,128]{1,0:T(8,128)S(1)} custom-call(f32[128,128]{1,0:T(8,128)S(1)} %convolution_subtract_fusion.5), custom_call_target="Cholesky" | custom-call | tf_op jit(solution)/shard_map/jit(cholesky)/cholesky | solution.py:70
  290.9 0.1 copy.46
  291.0 0.7 compare_reduce_fusion.1
  291.7 0.6 compare_reduce_fusion.2
  292.3 0.6 compare_reduce_fusion
  294.9 6.7 %while.16 = (s32[]{:T(128)}, f32[384,384]{0,1:T(8,128)S(1)}, s32[3,2]{0,1:T(2,128)S(1)}, f32[3,128,128]{2,1,0:T(8,128)S(1)}, s32[]{:T(128)}) while((s32[]{:T(128)}, f32[384,384]{0,1:T(8,128)S(1)}, s32[3,2]{0,1:T(2,128)S(1)}, f32[3,128,128]{2,1,0:T(8,128)S(1)}, s32[]{:T(128)}) %tuple.65), condition=%wide.while_cond, body=%wide.while_body.sunk | while | flops 2 | bytes 393321 | solution.py:72
  295.0 0.6 fusion.133
  295.6 1.4 dynamic-slice.7
  297.0 0.1 copy.53
  297.3 0.6 fusion.133
  297.9 1.4 dynamic-slice.7
  299.3 0.1 copy.53
  299.5 0.6 fusion.133
  300.1 1.4 dynamic-slice.7
  301.5 0.1 copy.53
  301.6 29.5 %custom-call.26 = f32[3,128,128]{1,2,0:T(8,128)S(1)} custom-call(f32[3,128,128]{2,1,0:T(8,128)S(1)} %get-tuple-element.141), custom_call_target="InvertDiagBlocksLowerTriangular" | custom-call | tf_op jit(solution)/shard_map/triangular_solve | solution.py:72
  331.2 0.3 fusion.100
  331.4 0.3 convolution_subtract_fusion.4
  331.7 0.3 fusion.106
  332.0 0.4 convolution_subtract_fusion.3
  332.4 0.3 fusion.108
  332.7 0.2 fusion.112
  332.9 0.2 convolution_subtract_fusion.2
  333.1 0.2 fusion.113
  333.4 0.3 convolution_subtract_fusion.1
  333.6 0.2 convolution_convert_fusion
  333.9 9.8 %all_gather.7 = bf16[384,1024]{1,0:T(8,128)(2,1)S(1)} all-gather(bf16[384,128]{1,0:T(8,128)(2,1)S(1)} %pad_maximum_fusion.1), channel_id=1, replica_groups=mesh['subj'=4,'vox'=8] {'vox'}, dimensions={1}, use_global_device_ids=true | all-gather | bytes 884736 | tf_op jit(solution)/shard_map/all_gather | solution.py:77
  343.7 4.4 %multiply_convert_fusion = bf16[2048,1024]{1,0:T(8,128)(2,1)} fusion(bf16[384,2048]{0,1:T(8,128)(2,1)S(1)} %bitcast.107, bf16[384,1024]{1,0:T(8,128)(2,1)S(1)} %all_gather.7), kind=kOutput, calls=%fused_computation.96 | convolution fusion | flops 1614807040 | bytes 6553600 | tf_op jit(solution)/shard_map/dot_general | solution.py:75
  (42 shorter events, 1.1 us)
Async XLA Ops:
  6.5 85.7 %all-gather.2.cloned.1.call-start = ((), (), s32[]{:S(2)}) async-start(), calls=%async_computation.1 | async-start | bytes 5242880 | tf_op jit(solution)/shard_map/all_gather | solution.py:42
  92.2 4.7 %copy-start.3 = (s32[1,8]{1,0:T(1,128)S(1)}, s32[1,8]{1,0:T(1,128)}, u32[]{:S(2)}) copy-start(s32[1,8]{1,0:T(1,128)} %param.12) | copy-start | bytes 100
  92.2 53.8 %all-to-all-start = ((bf16[512,8,512]{0,2,1:T(8,128)(2,1)}), bf16[512,8,512]{0,2,1:T(8,128)(2,1)}, u32[]{:S(2)}, u32[]{:S(2)}) async-start(bf16[512,8,512]{0,2,1:T(8,128)(2,1)} %bitcast.106), calls=%async_computation | async-start | bytes 8388608 | tf_op jit(solution)/shard_map/all_to_all | solution.py:43
  96.9 135.7 %all-reduce.7.cloned.1.call-start = ((), (), s32[]{:S(2)}) async-start(), calls=%async_computation.2 | async-start | bytes 1179648 | tf_op jit(solution)/shard_map/psum | solution.py:68
  152.5 4.6 %copy-start.2 = (s32[4096]{0:T(1024)S(1)}, s32[4096]{0:T(1024)}, u32[]{:S(2)}) copy-start(s32[4096]{0:T(1024)} %param.10) | copy-start | bytes 49156
  232.6 1.4 copy-start
  294.9 36.3 %copy-start.1 = (f32[1,384,128]{2,1,0:T(8,128)S(1)}, f32[1,384,128]{2,1,0:T(8,128)}, u32[]{:S(2)}) copy-start(f32[1,384,128]{2,1,0:T(8,128)} %param.14) | copy-start | bytes 589828
Sparse Core Ops, SparseCore 0:
  8.9 83.2 all-gather.1
  181.2 51.3 all-reduce.6
where the time goes:
time: 356 us; the launch traced here: 355 us
  waiting for transfers between devices  182 us (51%)
  other arithmetic  90.9 us (26%)
  local copies, waits for them, and re-layouts  23.6 us (7%)
  matrix products  21.5 us (6%)
  between operations  16.3 us (5%)
  blocking collectives  9.85 us (3%)
  loops' own time  6.06 us (2%)
  starting transfers between devices  4.72 us (1%)
    all_gather x1, waiting for transfers between devices, body(): grouped = lax.all_gather(features, 'subj', axis=0, tiled=True)  83.4 us
    another operation x11, other arithmetic, body(): factor = jnp.linalg.cholesky(system)  57 us
    psum x1, waiting for transfers between devices, body(): kernel = lax.psum(partial_kernel, 'vox') / (DELAYS * width)  49.8 us
    all_to_all x1, waiting for transfers between devices, body(): lax.all_to_all(grouped, 'vox', split_axis=1, concat_axis=0, tiled=True)  48.8 us
    another operation x4, other arithmetic, body(): lax.linalg.triangular_solve(factor, forward, left_side=True, lower=True,...  29.6 us
    dot_general x3, matrix products, interp_block(): jnp.dot(weights_table, shard_piece, preferred_element_type=jnp.float32)  11.5 us
    all_gather x1, blocking collectives, body(): lax.all_gather(dual_coef, 'vox', axis=1, tiled=True)  9.85 us
  transfers between devices with their start and end apart: 3, of which 3 were waited for; matrix products, arithmetic and copies ran while one was open for 0% of the time, Pallas kernels for 0%

commit v1 on v0

v1 whole, which is shorter than its diff:
```python
import functools

import jax
import jax.numpy as jnp
from jax import lax
from jax.experimental import pallas as pl
from jax.experimental.pallas import tpu as pltpu
from jax.sharding import PartitionSpec as P

DELAYS = 4
TICKS = 64
GAP = 6
BLOCK = 128
AXES = ("subj", "vox")
FULL = lax.Precision.HIGHEST
MESH = pl.DeviceIdType.MESH


def lanczos_rows(near_ticks, offset, tr_rows):
    distance = near_ticks[None, :] - (tr_rows[:, None] * TICKS + offset)
    inside = jnp.abs(distance) < 3 * TICKS
    scaled = distance.astype(jnp.float32) / TICKS
    shaped = jnp.sinc(scaled) * jnp.sinc(scaled / 3.0)
    return jnp.where(inside, shaped, jnp.zeros_like(shaped)).astype(jnp.bfloat16)


def delay_stack(interp, lengths, tr_total):
    starts = jnp.cumsum(lengths) - lengths
    tr_steps = jnp.arange(tr_total, dtype=jnp.int32)
    run_first = jnp.max(jnp.where(starts[None, :] <= tr_steps[:, None], starts[None, :], 0), axis=1)
    delayed = []
    for delay_step in range(1, DELAYS + 1):
        moved = jnp.concatenate(
            [jnp.zeros((delay_step, interp.shape[1]), interp.dtype), interp[:-delay_step]], axis=0
        )
        keep_rows = (tr_steps - delay_step >= run_first)[:, None]
        delayed.append(jnp.where(keep_rows, moved, jnp.zeros_like(moved)))
    return jnp.concatenate(delayed, axis=1)


def gram_kernel(n, scale, stacked_ref, out_ref, part, land, send_a, recv_a, send_b, recv_b):
    me = lax.axis_index("vox")
    total = out_ref.shape[0]
    rows = total // n
    barrier = pltpu.get_barrier_semaphore()
    for step in range(1, n):
        pl.semaphore_signal(
            barrier, inc=1, device_id={"vox": lax.rem(me + step, n)}, device_id_type=MESH
        )

    @pl.loop(0, total // BLOCK)
    def _(block):
        here = pl.ds(pl.multiple_of(block * BLOCK, BLOCK), BLOCK)
        part[here, :] = lax.dot_general(
            stacked_ref[here, :], stacked_ref[...], (((1,), (1,)), ((), ())),
            preferred_element_type=jnp.float32,
        )

    pl.semaphore_wait(barrier, n - 1)

    def rows_of(owner):
        return pl.ds(pl.multiple_of(owner * rows, rows), rows)

    def share(step):
        peer = lax.rem(me + step, n)
        return pltpu.make_async_remote_copy(
            src_ref=part.at[rows_of(peer), :], dst_ref=land.at[me],
            send_sem=send_a.at[step], recv_sem=recv_a.at[me],
            device_id={"vox": peer}, device_id_type=MESH,
        )

    def arrived(step):
        peer = lax.rem(me + step, n)
        return pltpu.make_async_remote_copy(
            src_ref=part.at[rows_of(me), :], dst_ref=land.at[peer],
            send_sem=send_a.at[step], recv_sem=recv_a.at[peer],
            device_id={"vox": peer}, device_id_type=MESH,
        )

    def spread(step):
        peer = lax.rem(me + step, n)
        return pltpu.make_async_remote_copy(
            src_ref=out_ref.at[rows_of(me), :], dst_ref=out_ref.at[rows_of(me), :],
            send_sem=send_b.at[step], recv_sem=recv_b.at[me],
            device_id={"vox": peer}, device_id_type=MESH,
        )

    def spread_in(step):
        peer = lax.rem(me + step, n)
        return pltpu.make_async_remote_copy(
            src_ref=out_ref.at[rows_of(peer), :], dst_ref=out_ref.at[rows_of(peer), :],
            send_sem=send_b.at[step], recv_sem=recv_b.at[peer],
            device_id={"vox": peer}, device_id_type=MESH,
        )

    for step in range(1, n):
        share(step).start()
    total_rows = part[rows_of(me), :]
    for step in range(1, n):
        arrived(step).wait_recv()
        total_rows = total_rows + land[lax.rem(me + step, n)]
    out_ref[rows_of(me), :] = total_rows * scale
    for step in range(1, n):
        spread(step).start()
    for step in range(1, n):
        spread_in(step).wait_recv()
    for step in range(1, n):
        share(step).wait_send()
        spread(step).wait_send()


def gram_sum(stacked, n, width):
    total = stacked.shape[0]
    rows = total // n
    return pl.pallas_call(
        functools.partial(gram_kernel, n, 1.0 / (DELAYS * width)),
        out_shape=jax.ShapeDtypeStruct((total, total), jnp.float32),
        in_specs=[pl.BlockSpec(memory_space=pltpu.VMEM)],
        out_specs=pl.BlockSpec(memory_space=pltpu.VMEM),
        scratch_shapes=[
            pltpu.VMEM((total, total), jnp.float32),
            pltpu.VMEM((n, rows, total), jnp.float32),
            pltpu.SemaphoreType.DMA((n,)),
            pltpu.SemaphoreType.DMA((n,)),
            pltpu.SemaphoreType.DMA((n,)),
            pltpu.SemaphoreType.DMA((n,)),
        ],
        compiler_params=pltpu.CompilerParams(
            collective_id=0, has_side_effects=True, vmem_limit_bytes=48 * 2**20
        ),
        name="gram_sum",
    )(stacked)


def full_dot(a, b):
    return jnp.dot(a, b, precision=FULL, preferred_element_type=jnp.float32)


def solve_kernel(kernel_ref, penalty_ref, targets_ref, out_ref, work, pair):
    total, voxels = targets_ref.shape
    blocks = total // BLOCK
    penalty = penalty_ref[0]
    row = lax.broadcasted_iota(jnp.int32, (BLOCK, BLOCK), 0)
    col = lax.broadcasted_iota(jnp.int32, (BLOCK, BLOCK), 1)
    eye = jnp.where(row == col, 1.0, 0.0).astype(jnp.float32)
    work[:, :total] = kernel_ref[...]
    work[:, total:] = targets_ref[...]
    for k in range(blocks):
        here = slice(k * BLOCK, (k + 1) * BLOCK)
        work[here, here] = work[here, here] + penalty * eye
    low = penalty * 0.9
    for k in range(blocks):
        here = slice(k * BLOCK, (k + 1) * BLOCK)
        after = (k + 1) * BLOCK
        diagonal = work[here, here]
        high = jnp.max(jnp.sum(jnp.abs(diagonal), axis=1))
        first = 2.0 / (low + high)
        pair[:BLOCK] = first * eye
        pair[BLOCK:] = first * diagonal

        def going(least):
            return least < 1.0 - 2.0**-12

        def step(least):
            inner = least * (2.0 - least)
            grow = 2.0 / (1.0 + inner)
            pair[...] = full_dot(pair[...], grow * (2.0 * eye - pair[BLOCK:]))
            return inner * grow

        lax.while_loop(going, step, low * first)
        inverse = pair[:BLOCK]
        inverse = inverse + full_dot(inverse, eye - full_dot(diagonal, inverse))
        ahead = full_dot(inverse, work[here, after:])
        work[here, after:] = ahead
        rest = blocks - 1 - k
        if 0 < rest <= 2:
            work[after:total, after:] -= full_dot(work[after:total, here], ahead)
        elif rest:

            @pl.loop(k + 1, blocks)
            def _(below):
                there = pl.ds(pl.multiple_of(below * BLOCK, BLOCK), BLOCK)
                work[there, after:] -= full_dot(work[there, here], work[here, after:])

    for k in range(blocks - 2, -1, -1):
        here = slice(k * BLOCK, (k + 1) * BLOCK)
        after = (k + 1) * BLOCK
        work[here, total:] -= full_dot(work[here, after:total], work[after:total, total:])
    out_ref[...] = work[:, total:].astype(out_ref.dtype)


def solve(kernel, penalty, targets):
    total, voxels = targets.shape
    return pl.pallas_call(
        solve_kernel,
        out_shape=jax.ShapeDtypeStruct((total, voxels), jnp.bfloat16),
        in_specs=[
            pl.BlockSpec(memory_space=pltpu.VMEM),
            pl.BlockSpec(memory_space=pltpu.SMEM),
            pl.BlockSpec(memory_space=pltpu.VMEM),
        ],
        out_specs=pl.BlockSpec(memory_space=pltpu.VMEM),
        scratch_shapes=[
            pltpu.VMEM((total, total + voxels), jnp.float32),
            pltpu.VMEM((2 * BLOCK, BLOCK), jnp.float32),
        ],
        compiler_params=pltpu.CompilerParams(vmem_limit_bytes=48 * 2**20),
        name="ridge_solve",
    )(kernel, penalty, targets)


def all_offsets(offsets):
    count = lax.axis_size("subj")
    found = [offsets]
    for turn in range(1, count):
        found.append(lax.ppermute(offsets, "subj", [(i, (i + turn) % count) for i in range(count)]))
    found = jnp.concatenate(found)
    mine = lax.axis_index("subj")
    order = lax.rem(mine - jnp.arange(count, dtype=jnp.int32) + count, count)
    pick = order[:, None] == jnp.arange(count, dtype=jnp.int32)[None, :]
    return jnp.sum(jnp.where(pick, found[None, :], 0), axis=1)


def body(features, token_ticks, offsets, run_lengths, penalty, responses):
    tok_dev, width = features.shape
    group_count = lax.axis_size("subj")
    vox_count = lax.axis_size("vox")
    devices = group_count * vox_count
    slab_width = width // vox_count
    rows_dev = tok_dev * GAP // TICKS
    tr_total = rows_dev * devices
    halo = 3 * TICKS // GAP
    spread = (GAP / TICKS) ** 0.5
    me = lax.axis_index("subj") * vox_count + lax.axis_index("vox")

    before = lax.ppermute(features[-halo:], AXES, [(i, i + 1) for i in range(devices - 1)])
    behind = lax.ppermute(features[:halo], AXES, [(i + 1, i) for i in range(devices - 1)])
    offset_list = all_offsets(offsets)
    far = jnp.full((halo,), -(2**20), jnp.int32)
    padded = jnp.concatenate([far, token_ticks, far])
    near_ticks = lax.dynamic_slice_in_dim(padded, me * tok_dev, tok_dev + 2 * halo, 0)
    tr_rows = me * rows_dev + jnp.arange(rows_dev, dtype=jnp.int32)
    table = jax.vmap(lambda offset: lanczos_rows(near_ticks, offset, tr_rows))(offset_list)
    table = table.reshape(group_count * rows_dev, tok_dev + 2 * halo)

    def term(part, tokens):
        return jnp.dot(part, tokens, preferred_element_type=jnp.float32)

    summed = term(table[:, halo:halo + tok_dev], features)
    summed = summed + term(table[:, :halo], before) + term(table[:, halo + tok_dev:], behind)
    mine = (summed * spread).astype(jnp.bfloat16)
    mine = mine.reshape(group_count, rows_dev, vox_count, slab_width).transpose(0, 2, 1, 3)
    mine = mine.reshape(devices, rows_dev, slab_width)
    interp = lax.all_to_all(mine, AXES, split_axis=0, concat_axis=0, tiled=True)
    interp = interp.reshape(tr_total, slab_width)

    stacked = delay_stack(interp, run_lengths[0], tr_total)
    kernel = gram_sum(stacked, vox_count, width)
    dual_coef = solve(kernel, penalty, responses[0])
    projected = lax.dot_general(
        stacked,
        lax.all_gather(dual_coef, "vox", axis=1, tiled=True),
        (((0,), (0,)), ((), ())),
        preferred_element_type=jnp.float32,
    )
    projected = (projected * (DELAYS * width) ** (-0.5)).astype(jnp.bfloat16)
    return projected.reshape(1, DELAYS, slab_width, projected.shape[1])


def solution(mesh):
    return jax.shard_map(
        body,
        mesh=mesh,
        in_specs=(
            P(("subj", "vox"), None),
            P(),
            P("subj"),
            P("subj", None),
            P("subj"),
            P("subj", None, "vox"),
        ),
        out_specs=P("subj", None, "vox", None),
        check_vma=False,
    )
```

time: 356 us -> 85.2 us (0.24)
  waiting for transfers between devices: 182 us -> 14.6 us
  other arithmetic: 90.9 us -> 3.49 us
  Pallas kernels: 0 us -> 27.7 us
  local copies, waits for them, and re-layouts: 23.6 us -> 3.12 us
  matrix products: 21.5 us -> 6.5 us
  between operations: 16.3 us -> 1.49 us
  starting transfers between devices: 4.72 us -> 16.6 us
  loops' own time: 6.06 us -> 0 us
    another operation x19 -> x1, other arithmetic: 87.5 us -> 0.18 us  [the longest x11 57 us: body(): factor = jnp.linalg.cholesky(system)]
    all_gather x1 -> x0, waiting for transfers between devices: 83.4 us -> none  [body(): grouped = lax.all_gather(features, 'subj', axis=0, tiled=True)]
    psum x1 -> x0, waiting for transfers between devices: 49.8 us -> none  [body(): kernel = lax.psum(partial_kernel, 'vox') / (DELAYS * width)]
    all_to_all x1, waiting for transfers between devices: 48.8 us -> 14.6 us  [body(): interp = lax.all_to_all(mine, AXES, split_axis=0, concat_axis=0, tiled=True)]
    pallas_call x0 -> x2, Pallas kernels: none -> 27.7 us  [the longest x1 17.1 us: gram_sum(): pl.pallas_call(functools.partial(gram_kernel, n, 1.0 / (DELAYS * width)),...]
    ppermute x0 -> x5, starting transfers between devices: none -> 12.2 us  [the longest x3 7.86 us: all_offsets(): lax.ppermute(offsets, 'subj', [(i, (i + turn) % count) for i in range(cou...]
    dot_general x4 -> x3, matrix products: 13.3 us -> 2.11 us  [term(): return jnp.dot(part, tokens, preferred_element_type=jnp.float32)]
    another operation x27 -> x0, local copies, waits for them, and re-layouts: 8.1 us -> none
  transfers between devices with their start and end apart: 3 -> 6, of which waited for: 3 -> 1; matrix products, arithmetic and copies ran while one was open for 0% -> 8% of each run, Pallas kernels for 0% -> 0%
where the time goes in v1:
time: 85.2 us; the launch traced here: 84.7 us
  Pallas kernels  27.7 us (33%)
  starting transfers between devices  16.6 us (19%)
  waiting for transfers between devices  14.6 us (17%)
  blocking collectives  11.2 us (13%)
  matrix products  6.5 us (8%)
  other arithmetic  3.49 us (4%)
  local copies, waits for them, and re-layouts  3.12 us (4%)
  between operations  1.49 us (2%)
    pallas_call x1, Pallas kernels, gram_sum(): pl.pallas_call(functools.partial(gram_kernel, n, 1.0 / (DELAYS * width)),...  17.1 us
    all_to_all x1, waiting for transfers between devices, body(): interp = lax.all_to_all(mine, AXES, split_axis=0, concat_axis=0, tiled=True)  14.6 us
    all_gather x1, blocking collectives, body(): lax.all_gather(dual_coef, 'vox', axis=1, tiled=True)  11.2 us
    pallas_call x1, Pallas kernels, solve(): pl.pallas_call(solve_kernel, out_shape=jax.ShapeDtypeStruct((total, voxel...  10.5 us
    ppermute x3, starting transfers between devices, all_offsets(): lax.ppermute(offsets, 'subj', [(i, (i + turn) % count) for i in range(cou...  7.86 us
    all_to_all x1, starting transfers between devices, body(): interp = lax.all_to_all(mine, AXES, split_axis=0, concat_axis=0, tiled=True)  4.43 us
    dot_general x1, matrix products, body(): lax.dot_general(stacked, lax.all_gather(dual_coef, 'vox', axis=1, tiled=T...  4.39 us
    ppermute x1, starting transfers between devices, body(): lax.ppermute(features[-halo:], AXES, [(i, i + 1) for i in range(devices -...  3.05 us
  transfers between devices with their start and end apart: 6, of which 1 were waited for; matrix products, arithmetic and copies ran while one was open for 8% of the time, Pallas kernels for 0%

profile of v1, /device:TPU:0, one launch (start us, length us, event | category | flops | bytes accessed | tf_op | source)
XLA Modules:
  0.0 84.7 jit_solution(74088313859350542)
XLA Ops:
  0.0 4.0 %collective-permute-start.1 = (s32[1]{0:T(128)}, s32[1]{0:T(128)}, u32[]{:S(2)}, u32[]{:S(2)}) collective-permute-start(s32[1]{0:T(128)} %param.9), channel_id=1, source_target_pairs={{0,16},{8,24},{16,0},{24,8},{1,17},{9,25},{17,1},{25,9},{2,18},{10... | collective-permute-start | bytes 20 | tf_op jit(solution)/shard_map/ppermute | solution.py:216
  4.0 1.6 %collective-permute-start = (s32[1]{0:T(128)}, s32[1]{0:T(128)}, u32[]{:S(2)}, u32[]{:S(2)}) collective-permute-start(s32[1]{0:T(128)} %param.9), channel_id=1, source_target_pairs={{0,8},{8,16},{16,24},{24,0},{1,9},{9,17},{17,25},{25,1},{2,10},{10... | collective-permute-start | bytes 20 | tf_op jit(solution)/shard_map/ppermute | solution.py:216
  5.6 2.2 %collective-permute-start.2 = (s32[1]{0:T(128)}, s32[1]{0:T(128)}, u32[]{:S(2)}, u32[]{:S(2)}) collective-permute-start(s32[1]{0:T(128)} %param.9), channel_id=1, source_target_pairs={{0,24},{8,0},{16,8},{24,16},{1,25},{9,1},{17,9},{25,17},{2,26},{10... | collective-permute-start | bytes 20 | tf_op jit(solution)/shard_map/ppermute | solution.py:216
  7.9 1.1 %fusion.51 = (bf16[32,4096]{1,0:T(8,128)(2,1)S(1)}, bf16[32,4096]{1,0:T(8,128)(2,1)S(1)}) fusion(bf16[128,4096]{1,0:T(8,128)(2,1)} %param.7), kind=kLoop, calls=%fused_computation.87 | loop fusion | bytes 1048576 | tf_op jit(solution)/shard_map/slice | solution.py:237
  8.9 1.3 %collective-permute-start.4 = (bf16[32,4096]{1,0:T(8,128)(2,1)S(1)}, bf16[32,4096]{1,0:T(8,128)(2,1)S(1)}, u32[]{:S(2)}, u32[]{:S(2)}) collective-permute-start(bf16[32,4096]{1,0:T(8,128)(2,1)S(1)} %get-tuple-element.6), channel_id=1, source_target_pairs={{1,0},{2,1},{3,2},{4,3},{5,4},{6,5},{7,6},{8,7},{9,8},{10,9},{11,1... | collective-permute-start | bytes 786440 | tf_op jit(solution)/shard_map/ppermute | solution.py:237
  10.2 3.0 %collective-permute-start.3 = (bf16[32,4096]{1,0:T(8,128)(2,1)S(1)}, bf16[32,4096]{1,0:T(8,128)(2,1)S(1)}, u32[]{:S(2)}, u32[]{:S(2)}) collective-permute-start(bf16[32,4096]{1,0:T(8,128)(2,1)S(1)} %get-tuple-element.7), channel_id=1, source_target_pairs={{0,1},{1,2},{2,3},{3,4},{4,5},{5,6},{6,7},{7,8},{8,9},{9,10},{10,1... | collective-permute-start | bytes 786440 | tf_op jit(solution)/shard_map/ppermute | solution.py:236
  14.0 0.8 concatenate.21
  14.8 0.1 dynamic_slice.3
  14.9 0.0 collective-permute-done.1
  14.9 0.0 collective-permute-done
  14.9 0.0 collective-permute-done.2
  14.9 1.9 %pad_add_fusion = s32[4]{0:T(128)S(1)} fusion(s32[1]{0:T(128)} %collective-permute-done.2, s32[1]{0:T(128)} %collective-permute-done.1, s32[1]{0:T(128)} %collective-permute-done, s32[1]{0:T(128)S(6)} %copy.11), kind=kLoop, calls=%fused_computation.84 | loop fusion | flops 12 | bytes 32 | tf_op jit(solution)/shard_map/concatenate | solution.py:217
  16.8 0.2 select_reduce_fusion.1
  17.0 0.1 broadcast_add_fusion
  17.1 0.2 fusion.45
  17.3 1.6 %fusion.48 = f32[48,4096]{1,0:T(8,128)S(1)} fusion(bf16[128,4096]{1,0:T(8,128)(2,1)} %param.7, bf16[48,192]{1,0:T(8,128)(2,1)S(1)} %reshape.102), kind=kOutput, calls=%fused_computation.70 | convolution fusion | flops 50331648 | bytes 1847296 | tf_op jit(solution)/shard_map/dot_general | solution.py:247
  18.9 0.0 copy-start.1
  18.9 0.0 collective-permute-done.3
  18.9 0.2 convolution_add_fusion.1
  19.2 0.0 collective-permute-done.4
  19.2 0.3 fusion.1
  19.5 0.1 copy.10
  19.6 0.9 %copy.9 = bf16[4,8,12,512]{3,2,1,0:T(8,128)(2,1)} copy(bf16[4,8,12,512]{3,1,2,0:T(8,128)(2,1)S(1)} %bitcast.23) | data formatting | bytes 786432 | tf_op jit(solution)/shard_map/transpose | solution.py:252
  20.6 4.4 %all-to-all-start = ((bf16[32,12,512]{2,1,0:T(8,128)(2,1)}), bf16[32,12,512]{2,1,0:T(8,128)(2,1)S(1)}, u32[]{:S(2)}, u32[]{:S(2)}) async-start(bf16[32,12,512]{2,1,0:T(8,128)(2,1)} %bitcast.2), calls=%async_computation | async-start | bytes 1048576 | tf_op jit(solution)/shard_map/all_to_all | solution.py:254
  25.7 0.0 copy-done.1
  25.7 0.2 reduce-window_clone.1
  25.9 0.1 select_reduce_fusion
  26.0 14.6 %all-to-all-done = bf16[32,12,512]{2,1,0:T(8,128)(2,1)S(1)} async-done(((bf16[32,12,512]{2,1,0:T(8,128)(2,1)}), bf16[32,12,512]{2,1,0:T(8,128)(2,1)S(1)}, u32[]{:S(2)}, u32[]{:S(2)}) %all-to-all-start) | async-done | bytes 393248 | tf_op jit(solution)/shard_map/all_to_all | solution.py:254
  40.6 0.1 reshape.105
  40.6 0.3 pad_select_fusion.2
  40.9 0.0 copy-start
  40.9 0.3 pad_select_fusion
  41.2 0.2 pad_maximum_fusion.stacked_ref
  41.4 17.1 %gram_sum.1.kernel_ref = f32[384,384]{1,0:T(8,128)S(1)} custom-call(bf16[384,2048]{1,0:T(8,128)(2,1)S(1)} %pad_maximum_fusion.stacked_ref), custom_call_target="tpu_custom_call" | custom-call | tf_op jit(solution)/shard_map/gram_sum/pallas_call | solution.py:115
  58.6 0.0 copy-done
  58.6 10.5 %ridge_solve.1 = bf16[384,128]{1,0:T(8,128)(2,1)S(1)} custom-call(f32[384,384]{1,0:T(8,128)S(1)} %gram_sum.1.kernel_ref, f32[1]{0:T(128)S(6)} %copy.12.penalty_ref, f32[384,128]{1,0:T(8,128)S(1)} %bitcast.18), custom_call_target="tpu_custom_call" | custom-call | tf_op jit(solution)/shard_map/ridge_solve/pallas_call | solution.py:194
  69.1 11.2 %all_gather.3 = bf16[384,1024]{1,0:T(8,128)(2,1)S(1)} all-gather(bf16[384,128]{1,0:T(8,128)(2,1)S(1)} %ridge_solve.1), channel_id=1, replica_groups=mesh['subj'=4,'vox'=8] {'vox'}, dimensions={1}, use_global_device_ids=true | all-gather | bytes 884736 | tf_op jit(solution)/shard_map/all_gather | solution.py:262
  80.3 4.4 %multiply_convert_fusion = bf16[2048,1024]{1,0:T(8,128)(2,1)} fusion(bf16[384,1024]{1,0:T(8,128)(2,1)S(1)} %all_gather.3, bf16[384,512]{1,0:T(8,128)(2,1)S(1)} %get-tuple-element.12, bf16[384,512]{1,0:T(8,128)(2,1)S(1)} %get-tuple-element.13, bf16[384,512]{1,0:T(8,128)(2,1)S(1)} %get-tuple-element.14, bf16[384,512]{1,0:T(8,128)(2,1)S(1)} %get-tuple-element.15), kind=kOutput, calls=%fused_computation | convolution fusion | flops 1621098496 | bytes 6553600 | tf_op jit(solution)/shard_map/dot_general | solution.py:260
  (6 shorter events, 0.1 us)
Async XLA Ops:
  0.0 14.9 %collective-permute-start.1 = (s32[1]{0:T(128)}, s32[1]{0:T(128)}, u32[]{:S(2)}, u32[]{:S(2)}) collective-permute-start(s32[1]{0:T(128)} %param.9), channel_id=1, source_target_pairs={{0,16},{8,24},{16,0},{24,8},{1,17},{9,25},{17,1},{25,9},{2,18},{10... | collective-permute-start | bytes 20 | tf_op jit(solution)/shard_map/ppermute | solution.py:216
  4.0 10.8 %collective-permute-start = (s32[1]{0:T(128)}, s32[1]{0:T(128)}, u32[]{:S(2)}, u32[]{:S(2)}) collective-permute-start(s32[1]{0:T(128)} %param.9), channel_id=1, source_target_pairs={{0,8},{8,16},{16,24},{24,0},{1,9},{9,17},{17,25},{25,1},{2,10},{10... | collective-permute-start | bytes 20 | tf_op jit(solution)/shard_map/ppermute | solution.py:216
  5.6 9.3 %collective-permute-start.2 = (s32[1]{0:T(128)}, s32[1]{0:T(128)}, u32[]{:S(2)}, u32[]{:S(2)}) collective-permute-start(s32[1]{0:T(128)} %param.9), channel_id=1, source_target_pairs={{0,24},{8,0},{16,8},{24,16},{1,25},{9,1},{17,9},{25,17},{2,26},{10... | collective-permute-start | bytes 20 | tf_op jit(solution)/shard_map/ppermute | solution.py:216
  8.9 10.2 %collective-permute-start.4 = (bf16[32,4096]{1,0:T(8,128)(2,1)S(1)}, bf16[32,4096]{1,0:T(8,128)(2,1)S(1)}, u32[]{:S(2)}, u32[]{:S(2)}) collective-permute-start(bf16[32,4096]{1,0:T(8,128)(2,1)S(1)} %get-tuple-element.6), channel_id=1, source_target_pairs={{1,0},{2,1},{3,2},{4,3},{5,4},{6,5},{7,6},{8,7},{9,8},{10,9},{11,1... | collective-permute-start | bytes 786440 | tf_op jit(solution)/shard_map/ppermute | solution.py:237
  10.2 8.7 %collective-permute-start.3 = (bf16[32,4096]{1,0:T(8,128)(2,1)S(1)}, bf16[32,4096]{1,0:T(8,128)(2,1)S(1)}, u32[]{:S(2)}, u32[]{:S(2)}) collective-permute-start(bf16[32,4096]{1,0:T(8,128)(2,1)S(1)} %get-tuple-element.7), channel_id=1, source_target_pairs={{0,1},{1,2},{2,3},{3,4},{4,5},{5,6},{6,7},{7,8},{8,9},{9,10},{10,1... | collective-permute-start | bytes 786440 | tf_op jit(solution)/shard_map/ppermute | solution.py:236
  18.9 6.7 %copy-start.1 = (s32[1,8]{1,0:T(1,128)S(1)}, s32[1,8]{1,0:T(1,128)}, u32[]{:S(2)}) copy-start(s32[1,8]{1,0:T(1,128)} %param.10) | copy-start | bytes 100
  20.6 20.0 %all-to-all-start = ((bf16[32,12,512]{2,1,0:T(8,128)(2,1)}), bf16[32,12,512]{2,1,0:T(8,128)(2,1)S(1)}, u32[]{:S(2)}, u32[]{:S(2)}) async-start(bf16[32,12,512]{2,1,0:T(8,128)(2,1)} %bitcast.2), calls=%async_computation | async-start | bytes 1048576 | tf_op jit(solution)/shard_map/all_to_all | solution.py:254
  40.9 17.7 %copy-start = (f32[1,384,128]{2,1,0:T(8,128)S(1)}, f32[1,384,128]{2,1,0:T(8,128)}, u32[]{:S(2)}) copy-start(f32[1,384,128]{2,1,0:T(8,128)} %param.12) | copy-start | bytes 589828

commit v2 on v1

--- a/solution.py
+++ b/solution.py
@@ -11,17 +11,8 @@
 TICKS = 64
 GAP = 6
 BLOCK = 128
-AXES = ("subj", "vox")
 FULL = lax.Precision.HIGHEST
 MESH = pl.DeviceIdType.MESH
-
-
-def lanczos_rows(near_ticks, offset, tr_rows):
-    distance = near_ticks[None, :] - (tr_rows[:, None] * TICKS + offset)
-    inside = jnp.abs(distance) < 3 * TICKS
-    scaled = distance.astype(jnp.float32) / TICKS
-    shaped = jnp.sinc(scaled) * jnp.sinc(scaled / 3.0)
-    return jnp.where(inside, shaped, jnp.zeros_like(shaped)).astype(jnp.bfloat16)
 
 
 def delay_stack(interp, lengths, tr_total):
@@ -36,6 +27,195 @@
         keep_rows = (tr_steps - delay_step >= run_first)[:, None]
         delayed.append(jnp.where(keep_rows, moved, jnp.zeros_like(moved)))
     return jnp.concatenate(delayed, axis=1)
+
+
+def sinc(x):
+    angle = jnp.pi * x
+    return jnp.where(x == 0, 1.0, jnp.sin(angle) / jnp.where(x == 0, 1.0, angle))
+
+
+def spread_kernel(groups, vox, rows_dev, scale, feat_ref, tick_ref, shift_ref, out_ref,
+                  edges, shifts, held, send_o, recv_o, send_e, recv_e, send_x, recv_x):
+    tok_dev, width = feat_ref.shape
+    slab = width // vox
+    halo = edges.shape[0] // 2
+    devices = groups * vox
+    my_group = lax.axis_index("subj")
+    my_vox = lax.axis_index("vox")
+    me = my_group * vox + my_vox
+
+    def place(device):
+        return {"subj": device // vox, "vox": lax.rem(device, vox)}
+
+    barrier = pltpu.get_barrier_semaphore()
+
+    @pl.loop(1, devices)
+    def _(turn):
+        pl.semaphore_signal(
+            barrier, inc=1, device_id=place(lax.rem(me + turn, devices)), device_id_type=MESH
+        )
+
+    shifts[my_group] = shift_ref[...]
+    pl.semaphore_wait(barrier, devices - 1)
+
+    def tell(turn):
+        return pltpu.make_async_remote_copy(
+            src_ref=shift_ref, dst_ref=shifts.at[my_group],
+            send_sem=send_o.at[turn], recv_sem=recv_o.at[my_group],
+            device_id={"subj": lax.rem(my_group + turn, groups)}, device_id_type=MESH,
+        )
+
+    def told(turn):
+        other = lax.rem(my_group + turn, groups)
+        return pltpu.make_async_remote_copy(
+            src_ref=shift_ref, dst_ref=shifts.at[other],
+            send_sem=send_o.at[turn], recv_sem=recv_o.at[other],
+            device_id={"subj": other}, device_id_type=MESH,
+        )
+
+    def upward(peer):
+        return pltpu.make_async_remote_copy(
+            src_ref=feat_ref.at[tok_dev - halo:, :], dst_ref=edges.at[:halo, :],
+            send_sem=send_e.at[0], recv_sem=recv_e.at[0],
+            device_id=place(peer), device_id_type=MESH,
+        )
+
+    def downward(peer):
+        return pltpu.make_async_remote_copy(
+            src_ref=feat_ref.at[:halo, :], dst_ref=edges.at[halo:, :],
+            send_sem=send_e.at[1], recv_sem=recv_e.at[1],
+            device_id=place(peer), device_id_type=MESH,
+        )
+
+    for turn in range(1, groups):
+        tell(turn).start()
+
+    @pl.when(me < devices - 1)
+    def _():
+        upward(me + 1).start()
+
+    @pl.when(me > 0)
+    def _():
+        downward(me - 1).start()
+
+    @pl.when(me == 0)
+    def _():
+        edges[:halo, :] = jnp.zeros((halo, width), edges.dtype)
+
+    @pl.when(me == devices - 1)
+    def _():
+        edges[halo:, :] = jnp.zeros((halo, width), edges.dtype)
+
+    for turn in range(1, groups):
+        told(turn).wait_recv()
+    near = tick_ref[0:1, :]
+    first = (me * rows_dev + lax.broadcasted_iota(jnp.int32, (16, near.shape[1]), 0)) * TICKS
+    pieces = []
+    for group in range(groups):
+        distance = near - (first + shifts[group][0:1, :])
+        inside = jnp.abs(distance) < 3 * TICKS
+        scaled = distance.astype(jnp.float32) / TICKS
+        shaped = sinc(scaled) * sinc(scaled / 3.0)
+        pieces.append(jnp.where(inside, shaped, jnp.zeros_like(shaped)))
+    table = jnp.concatenate(pieces, axis=0).astype(jnp.bfloat16)
+    inner = table[:, :tok_dev]
+    outer = table[:, tok_dev:tok_dev + 2 * halo]
+
+    @pl.when(me > 0)
+    def _():
+        upward(me - 1).wait_recv()
+
+    @pl.when(me < devices - 1)
+    def _():
+        downward(me + 1).wait_recv()
+
+    def columns(index):
+        return pl.ds(pl.multiple_of(index * slab, slab), slab)
+
+    def rows(index):
+        return pl.ds(pl.multiple_of(index * 16, 16), 16)
+
+    def give(group, index):
+        return pltpu.make_async_remote_copy(
+            src_ref=held.at[rows(group), columns(index)], dst_ref=out_ref.at[rows(me), :],
+            send_sem=send_x.at[group * vox + index], recv_sem=recv_x.at[me],
+            device_id={"subj": group, "vox": index}, device_id_type=MESH,
+        )
+
+    def taken(source):
+        return pltpu.make_async_remote_copy(
+            src_ref=held.at[rows(0), columns(0)], dst_ref=out_ref.at[rows(source), :],
+            send_sem=send_x.at[source], recv_sem=recv_x.at[source],
+            device_id=place(source), device_id_type=MESH,
+        )
+
+    def make(index):
+        summed = jnp.dot(inner, feat_ref[:, columns(index)], preferred_element_type=jnp.float32)
+        summed = summed + jnp.dot(
+            outer, edges[:, columns(index)], preferred_element_type=jnp.float32
+        )
+        held[:, columns(index)] = (summed * scale).astype(jnp.bfloat16)
+
+    @pl.loop(1, vox)
+    def _(step):
+        index = lax.rem(my_vox + step, vox)
+        make(index)
+        for turn in range(groups):
+            give(lax.rem(my_group + turn, groups), index).start()
+
+    make(my_vox)
+    for turn in range(1, groups):
+        give(lax.rem(my_group + turn, groups), my_vox).start()
+    out_ref[rows(me), :] = held[rows(my_group), columns(my_vox)]
+
+    @pl.loop(1, devices)
+    def _(turn):
+        other = lax.rem(me + turn, devices)
+        taken(other).wait_recv()
+
+    @pl.loop(1, devices)
+    def _(turn):
+        other = lax.rem(me + turn, devices)
+        give(other // vox, lax.rem(other, vox)).wait_send()
+
+    for turn in range(1, groups):
+        tell(turn).wait_send()
+
+    @pl.when(me < devices - 1)
+    def _():
+        upward(me + 1).wait_send()
+
+    @pl.when(me > 0)
+    def _():
+        downward(me - 1).wait_send()
+
+
+def spread_interp(features, ticks, shift, groups, vox, rows_dev, halo):
+    tok_dev, width = features.shape
+    devices = groups * vox
+    slab = width // vox
+    lanes = ticks.shape[1]
+    return pl.pallas_call(
+        functools.partial(spread_kernel, groups, vox, rows_dev, (GAP / TICKS) ** 0.5),
+        out_shape=jax.ShapeDtypeStruct((devices * 16, slab), jnp.bfloat16),
+        in_specs=[pl.BlockSpec(memory_space=pltpu.VMEM)] * 3,
+        out_specs=pl.BlockSpec(memory_space=pltpu.VMEM),
+        scratch_shapes=[
+            pltpu.VMEM((2 * halo, width), jnp.bfloat16),
+            pltpu.VMEM((groups, 8, lanes), jnp.int32),
+            pltpu.VMEM((groups * 16, width), jnp.bfloat16),
+            pltpu.SemaphoreType.DMA((groups,)),
+            pltpu.SemaphoreType.DMA((groups,)),
+            pltpu.SemaphoreType.DMA((2,)),
+            pltpu.SemaphoreType.DMA((2,)),
+            pltpu.SemaphoreType.DMA((devices,)),
+            pltpu.SemaphoreType.DMA((devices,)),
+        ],
+        compiler_params=pltpu.CompilerParams(
+            collective_id=1, has_side_effects=True, vmem_limit_bytes=32 * 2**20
+        ),
+        name="spread_interp",
+    )(features, ticks, shift)
 
 
 def gram_kernel(n, scale, stacked_ref, out_ref, part, land, send_a, recv_a, send_b, recv_b):
@@ -209,18 +389,6 @@
     )(kernel, penalty, targets)
 
 
-def all_offsets(offsets):
-    count = lax.axis_size("subj")
-    found = [offsets]
-    for turn in range(1, count):
-        found.append(lax.ppermute(offsets, "subj", [(i, (i + turn) % count) for i in range(count)]))
-    found = jnp.concatenate(found)
-    mine = lax.axis_index("subj")
-    order = lax.rem(mine - jnp.arange(count, dtype=jnp.int32) + count, count)
-    pick = order[:, None] == jnp.arange(count, dtype=jnp.int32)[None, :]
-    return jnp.sum(jnp.where(pick, found[None, :], 0), axis=1)
-
-
 def body(features, token_ticks, offsets, run_lengths, penalty, responses):
     tok_dev, width = features.shape
     group_count = lax.axis_size("subj")
@@ -230,29 +398,18 @@
     rows_dev = tok_dev * GAP // TICKS
     tr_total = rows_dev * devices
     halo = 3 * TICKS // GAP
-    spread = (GAP / TICKS) ** 0.5
     me = lax.axis_index("subj") * vox_count + lax.axis_index("vox")
 
-    before = lax.ppermute(features[-halo:], AXES, [(i, i + 1) for i in range(devices - 1)])
-    behind = lax.ppermute(features[:halo], AXES, [(i + 1, i) for i in range(devices - 1)])
-    offset_list = all_offsets(offsets)
-    far = jnp.full((halo,), -(2**20), jnp.int32)
+    far = jnp.full((tok_dev,), -(2**20), jnp.int32)
     padded = jnp.concatenate([far, token_ticks, far])
-    near_ticks = lax.dynamic_slice_in_dim(padded, me * tok_dev, tok_dev + 2 * halo, 0)
-    tr_rows = me * rows_dev + jnp.arange(rows_dev, dtype=jnp.int32)
-    table = jax.vmap(lambda offset: lanczos_rows(near_ticks, offset, tr_rows))(offset_list)
-    table = table.reshape(group_count * rows_dev, tok_dev + 2 * halo)
-
-    def term(part, tokens):
-        return jnp.dot(part, tokens, preferred_element_type=jnp.float32)
-
-    summed = term(table[:, halo:halo + tok_dev], features)
-    summed = summed + term(table[:, :halo], before) + term(table[:, halo + tok_dev:], behind)
-    mine = (summed * spread).astype(jnp.bfloat16)
-    mine = mine.reshape(group_count, rows_dev, vox_count, slab_width).transpose(0, 2, 1, 3)
-    mine = mine.reshape(devices, rows_dev, slab_width)
-    interp = lax.all_to_all(mine, AXES, split_axis=0, concat_axis=0, tiled=True)
-    interp = interp.reshape(tr_total, slab_width)
+    near = lax.dynamic_slice_in_dim(padded, me * tok_dev + tok_dev - halo, tok_dev + 2 * halo, 0)
+    ticks = jnp.concatenate(
+        [near[halo:halo + tok_dev], near[:halo], near[halo + tok_dev:], far[:tok_dev - 2 * halo]]
+    )
+    ticks = jnp.broadcast_to(ticks, (8, 2 * tok_dev))
+    shift = jnp.broadcast_to(offsets[0], (8, 2 * tok_dev))
+    blocks = spread_interp(features, ticks, shift, group_count, vox_count, rows_dev, halo)
+    interp = blocks.reshape(devices, 16, slab_width)[:, :rows_dev].reshape(tr_total, slab_width)
 
     stacked = delay_stack(interp, run_lengths[0], tr_total)
     kernel = gram_sum(stacked, vox_count, width)

time: 85.2 us -> 79 us (0.927)
  Pallas kernels: 27.7 us -> 57.4 us
  starting transfers between devices: 16.6 us -> 0 us
  waiting for transfers between devices: 14.6 us -> 0 us
  matrix products: 6.5 us -> 4.39 us
  local copies, waits for them, and re-layouts: 3.12 us -> 1.47 us
    pallas_call x0 -> x1, Pallas kernels: none -> 27.4 us  [spread_interp(): pl.pallas_call(functools.partial(spread_kernel, groups, vox, rows_dev, (G...]
    all_to_all x1 -> x0, waiting for transfers between devices: 14.6 us -> none  [body(): interp = lax.all_to_all(mine, AXES, split_axis=0, concat_axis=0, tiled=True)]
    ppermute x5 -> x0, starting transfers between devices: 12.2 us -> none  [the longest x3 7.86 us: all_offsets(): lax.ppermute(offsets, 'subj', [(i, (i + turn) % count) for i in range(cou...]
    all_to_all x1 -> x0, starting transfers between devices: 4.43 us -> none  [body(): interp = lax.all_to_all(mine, AXES, split_axis=0, concat_axis=0, tiled=True)]
    dot_general x3 -> x0, matrix products: 2.11 us -> none  [term(): return jnp.dot(part, tokens, preferred_element_type=jnp.float32)]
    pallas_call x1, Pallas kernels: 10.5 us -> 12 us  [solve(): pl.pallas_call(solve_kernel, out_shape=jax.ShapeDtypeStruct((total, voxel...]
    unnamed x5 -> x4, local copies, waits for them, and re-layouts: 0.14 us -> 1.23 us
    concatenate x1 -> x2, other arithmetic: 1.94 us -> 0.86 us  [the longest x1 0.78 us: body(): padded = jnp.concatenate([far, token_ticks, far])]
  transfers between devices with their start and end apart: 6 -> 0, of which waited for: 1 -> 0; matrix products, arithmetic and copies ran while one was open for 8% -> 0% of each run, Pallas kernels for 0% -> 0%
where the time goes in v2:
time: 79 us; the launch traced here: 78.9 us
  Pallas kernels  57.4 us (73%)
  blocking collectives  11.1 us (14%)
  matrix products  4.39 us (6%)
  other arithmetic  3.19 us (4%)
  local copies, waits for them, and re-layouts  1.47 us (2%)
  between operations  1.39 us (2%)
    pallas_call x1, Pallas kernels, spread_interp(): pl.pallas_call(functools.partial(spread_kernel, groups, vox, rows_dev, (G...  27.4 us
    pallas_call x1, Pallas kernels, gram_sum(): pl.pallas_call(functools.partial(gram_kernel, n, 1.0 / (DELAYS * width)),...  17.9 us
    pallas_call x1, Pallas kernels, solve(): pl.pallas_call(solve_kernel, out_shape=jax.ShapeDtypeStruct((total, voxel...  12 us
    all_gather x1, blocking collectives, body(): lax.all_gather(dual_coef, 'vox', axis=1, tiled=True)  11.1 us
    dot_general x1, matrix products, body(): lax.dot_general(stacked, lax.all_gather(dual_coef, 'vox', axis=1, tiled=T...  4.39 us

profile of v2, /device:TPU:0, one launch (start us, length us, event | category | flops | bytes accessed | tf_op | source)
XLA Modules:
  0.0 78.9 jit_solution(16304905172650317608)
XLA Ops:
  1.3 0.8 %reduce-window_clone.1 = s32[1,8]{1,0:T(1,128)S(1)} reduce-window(s32[1,8]{1,0:T(1,128)} %param.9, s32[]{:T(128)} %constant.16.clone.1), window={size=1x8 pad=0_0x7_0}, to_apply=%region_0.0 | reduce-window | flops 56 | bytes 68 | tf_op jit(solution)/shard_map/reduce-window.clone
  2.1 0.7 subtract_bitcast_fusion
  2.8 0.8 fusion.1
  3.6 0.1 slice.27
  3.6 0.1 fusion.2
  3.7 0.1 pad_add_fusion
  3.8 0.1 select_reduce_fusion
  3.9 0.0 copy-start
  3.9 1.2 %copy-done = bf16[128,4096]{1,0:T(8,128)(2,1)S(1)} copy-done((bf16[128,4096]{1,0:T(8,128)(2,1)S(1)}, bf16[128,4096]{1,0:T(8,128)(2,1)}, u32[]{:S(2)}) %copy-start) | copy-done | bytes 1048600
  5.1 27.4 %spread_interp.1 = bf16[512,512]{1,0:T(8,128)(2,1)S(1)} custom-call(bf16[128,4096]{1,0:T(8,128)(2,1)S(1)} %copy-done, s32[8,256]{1,0:T(8,128)S(1)} %broadcast_in_dim.56.tick_ref, s32[8,256]{1,0:T(8,128)S(1)} %broadcast_in_dim.57.shift_ref), custom_call_target="tpu_custom_call" | custom-call | tf_op jit(solution)/shard_map/spread_interp/pallas_call | solution.py:198
  32.6 0.1 reshape.44
  32.7 0.3 pad_select_fusion.2
  33.0 0.0 copy-start.1
  33.0 0.3 pad_select_fusion
  33.2 0.2 pad_maximum_fusion.stacked_ref
  33.5 17.9 %gram_sum.1.kernel_ref = f32[384,384]{1,0:T(8,128)S(1)} custom-call(bf16[384,2048]{1,0:T(8,128)(2,1)S(1)} %pad_maximum_fusion.stacked_ref), custom_call_target="tpu_custom_call" | custom-call | tf_op jit(solution)/shard_map/gram_sum/pallas_call | solution.py:295
  51.4 0.0 copy-done.1
  51.4 12.0 %ridge_solve.1 = bf16[384,128]{1,0:T(8,128)(2,1)S(1)} custom-call(f32[384,384]{1,0:T(8,128)S(1)} %gram_sum.1.kernel_ref, f32[1]{0:T(128)S(6)} %copy.8.penalty_ref, f32[384,128]{1,0:T(8,128)S(1)} %bitcast.14), custom_call_target="tpu_custom_call" | custom-call | tf_op jit(solution)/shard_map/ridge_solve/pallas_call | solution.py:374
  63.4 11.1 %all_gather.3 = bf16[384,1024]{1,0:T(8,128)(2,1)S(1)} all-gather(bf16[384,128]{1,0:T(8,128)(2,1)S(1)} %ridge_solve.1), channel_id=1, replica_groups=mesh['subj'=4,'vox'=8] {'vox'}, dimensions={1}, use_global_device_ids=true | all-gather | bytes 884736 | tf_op jit(solution)/shard_map/all_gather | solution.py:419
  74.5 4.4 %multiply_convert_fusion = bf16[2048,1024]{1,0:T(8,128)(2,1)} fusion(bf16[384,1024]{1,0:T(8,128)(2,1)S(1)} %all_gather.3, bf16[384,512]{1,0:T(8,128)(2,1)S(1)} %get-tuple-element.11, bf16[384,512]{1,0:T(8,128)(2,1)S(1)} %get-tuple-element.12, bf16[384,512]{1,0:T(8,128)(2,1)S(1)} %get-tuple-element.13, bf16[384,512]{1,0:T(8,128)(2,1)S(1)} %get-tuple-element.14), kind=kOutput, calls=%fused_computation | convolution fusion | flops 1621098496 | bytes 6553600 | tf_op jit(solution)/shard_map/dot_general | solution.py:417
  (5 shorter events, 0.0 us)
Async XLA Ops:
  3.9 1.2 %copy-start = (bf16[128,4096]{1,0:T(8,128)(2,1)S(1)}, bf16[128,4096]{1,0:T(8,128)(2,1)}, u32[]{:S(2)}) copy-start(bf16[128,4096]{1,0:T(8,128)(2,1)} %feat_ref.1) | copy-start | bytes 3145732
  33.0 18.5 %copy-start.1 = (f32[1,384,128]{2,1,0:T(8,128)S(1)}, f32[1,384,128]{2,1,0:T(8,128)}, u32[]{:S(2)}) copy-start(f32[1,384,128]{2,1,0:T(8,128)} %param.11) | copy-start | bytes 589828

commit v3 on v2

--- a/solution.py
+++ b/solution.py
@@ -16,7 +16,8 @@
 
 
 def delay_stack(interp, lengths, tr_total):
-    starts = jnp.cumsum(lengths) - lengths
+    runs = jnp.arange(lengths.shape[0])
+    starts = jnp.sum(jnp.where(runs[None, :] < runs[:, None], lengths[None, :], 0), axis=1)
     tr_steps = jnp.arange(tr_total, dtype=jnp.int32)
     run_first = jnp.max(jnp.where(starts[None, :] <= tr_steps[:, None], starts[None, :], 0), axis=1)
     delayed = []
@@ -316,15 +317,11 @@
     return jnp.dot(a, b, precision=FULL, preferred_element_type=jnp.float32)
 
 
-def solve_kernel(kernel_ref, penalty_ref, targets_ref, out_ref, work, pair):
-    total, voxels = targets_ref.shape
+def ridge(work, pair, total, penalty):
     blocks = total // BLOCK
-    penalty = penalty_ref[0]
     row = lax.broadcasted_iota(jnp.int32, (BLOCK, BLOCK), 0)
     col = lax.broadcasted_iota(jnp.int32, (BLOCK, BLOCK), 1)
     eye = jnp.where(row == col, 1.0, 0.0).astype(jnp.float32)
-    work[:, :total] = kernel_ref[...]
-    work[:, total:] = targets_ref[...]
     for k in range(blocks):
         here = slice(k * BLOCK, (k + 1) * BLOCK)
         work[here, here] = work[here, here] + penalty * eye
@@ -365,28 +362,96 @@
     for k in range(blocks - 2, -1, -1):
         here = slice(k * BLOCK, (k + 1) * BLOCK)
         after = (k + 1) * BLOCK
-        work[here, total:] -= full_dot(work[here, after:total], work[after:total, total:])
+        if blocks - 1 - k <= 2:
+            work[here, total:] -= full_dot(work[here, after:total], work[after:total, total:])
+        else:
+            for below in range(k + 1, blocks):
+                there = slice(below * BLOCK, (below + 1) * BLOCK)
+                work[here, total:] -= full_dot(work[here, there], work[there, total:])
+
+
+def fetch_all(kernel_ref, targets_ref, work, fetched):
+    parts, total, voxels = targets_ref.shape
+    fetches = [pltpu.make_async_copy(kernel_ref, work.at[:, :total], fetched.at[parts])]
+    for part in range(parts):
+        columns = slice(total + part * voxels, total + (part + 1) * voxels)
+        fetches.append(
+            pltpu.make_async_copy(targets_ref.at[part], work.at[:, columns], fetched.at[part])
+        )
+    for fetch in fetches:
+        fetch.start()
+    for fetch in fetches:
+        fetch.wait()
+
+
+def dual_kernel(kernel_ref, penalty_ref, targets_ref, out_ref, work, pair, fetched):
+    total = targets_ref.shape[1]
+    fetch_all(kernel_ref, targets_ref, work, fetched)
+    ridge(work, pair, total, penalty_ref[0])
     out_ref[...] = work[:, total:].astype(out_ref.dtype)
 
 
-def solve(kernel, penalty, targets):
+def solve_kernel(scale, kernel_ref, penalty_ref, targets_ref, stacked_ref, out_ref,
+                 work, pair, dual, result, done, fetched):
+    total = targets_ref.shape[1]
+    fetch_all(kernel_ref, targets_ref, work, fetched)
+    ridge(work, pair, total, penalty_ref[0])
+    dual[...] = work[:, total:].astype(dual.dtype)
+    slab = result.shape[1]
+
+    def leave(step):
+        return pltpu.make_async_copy(result.at[step], out_ref.at[0, step], done.at[step])
+
+    for step in range(DELAYS):
+        projected = lax.dot_general(
+            stacked_ref[:, step * slab:(step + 1) * slab], dual[...], (((0,), (0,)), ((), ())),
+            preferred_element_type=jnp.float32,
+        )
+        result[step] = (projected * scale).astype(result.dtype)
+        leave(step).start()
+    for step in range(DELAYS):
+        leave(step).wait()
+
+
+def solve_dual(kernel, penalty, targets):
     total, voxels = targets.shape
+    away = pl.BlockSpec(memory_space=pl.ANY)
     return pl.pallas_call(
-        solve_kernel,
+        dual_kernel,
         out_shape=jax.ShapeDtypeStruct((total, voxels), jnp.bfloat16),
-        in_specs=[
-            pl.BlockSpec(memory_space=pltpu.VMEM),
-            pl.BlockSpec(memory_space=pltpu.SMEM),
-            pl.BlockSpec(memory_space=pltpu.VMEM),
-        ],
+        in_specs=[away, pl.BlockSpec(memory_space=pltpu.SMEM), away],
         out_specs=pl.BlockSpec(memory_space=pltpu.VMEM),
         scratch_shapes=[
             pltpu.VMEM((total, total + voxels), jnp.float32),
             pltpu.VMEM((2 * BLOCK, BLOCK), jnp.float32),
+            pltpu.SemaphoreType.DMA((2,)),
         ],
         compiler_params=pltpu.CompilerParams(vmem_limit_bytes=48 * 2**20),
+        name="ridge_dual",
+    )(kernel, penalty, targets[None])
+
+
+def solve(kernel, penalty, targets, stacked, width):
+    parts, total, voxels = targets.shape
+    slab = stacked.shape[1] // DELAYS
+    block = pl.BlockSpec(memory_space=pltpu.VMEM)
+    away = pl.BlockSpec(memory_space=pl.ANY)
+    return pl.pallas_call(
+        functools.partial(solve_kernel, (DELAYS * width) ** (-0.5)),
+        out_shape=jax.ShapeDtypeStruct((1, DELAYS, slab, parts * voxels), jnp.bfloat16),
+        in_specs=[away, pl.BlockSpec(memory_space=pltpu.SMEM), away, block],
+        out_specs=pl.BlockSpec(memory_space=pl.ANY),
+        scratch_shapes=[
+            pltpu.VMEM((total, total + parts * voxels), jnp.float32),
+            pltpu.VMEM((2 * BLOCK, BLOCK), jnp.float32),
+            pltpu.VMEM((total, parts * voxels), jnp.bfloat16),
+            pltpu.VMEM((DELAYS, slab, parts * voxels), jnp.bfloat16),
+            pltpu.SemaphoreType.DMA((DELAYS,)),
+            pltpu.SemaphoreType.DMA((parts + 1,)),
+        ],
+        compiler_params=pltpu.CompilerParams(vmem_limit_bytes=60 * 2**20),
         name="ridge_solve",
-    )(kernel, penalty, targets)
+    )(kernel, penalty, targets, stacked)
 
 
 def body(features, token_ticks, offsets, run_lengths, penalty, responses):
@@ -399,6 +464,9 @@
     tr_total = rows_dev * devices
     halo = 3 * TICKS // GAP
     me = lax.axis_index("subj") * vox_count + lax.axis_index("vox")
+    whole = tr_total <= 4 * BLOCK
+    if whole:
+        targets = lax.all_gather(responses[0], "vox", axis=0)
 
     far = jnp.full((tok_dev,), -(2**20), jnp.int32)
     padded = jnp.concatenate([far, token_ticks, far])
@@ -413,7 +481,9 @@
 
     stacked = delay_stack(interp, run_lengths[0], tr_total)
     kernel = gram_sum(stacked, vox_count, width)
-    dual_coef = solve(kernel, penalty, responses[0])
+    if whole:
+        return solve(kernel, penalty, targets, stacked, width)
+    dual_coef = solve_dual(kernel, penalty, responses[0])
     projected = lax.dot_general(
         stacked,
         lax.all_gather(dual_coef, "vox", axis=1, tiled=True),

time: 79 us -> 87.4 us (1.11); the launches traced: 78.9 us -> 86.2 us
  between operations: 1.39 us -> 14.8 us
  blocking collectives: 11.1 us -> 0 us
  Pallas kernels: 57.4 us -> 65.9 us
  matrix products: 4.39 us -> 0 us
    all_gather x1 -> x0, blocking collectives: 11.1 us -> none  [body(): lax.all_gather(dual_coef, 'vox', axis=1, tiled=True)]
    pallas_call x1, Pallas kernels: 12 us -> 19.7 us  [solve(): pl.pallas_call(functools.partial(solve_kernel, (DELAYS * width) ** (-0.5)...]
    dot_general x1 -> x0, matrix products: 4.39 us -> none  [body(): lax.dot_general(stacked, lax.all_gather(dual_coef, 'vox', axis=1, tiled=T...]
    unnamed x4 -> x6, local copies, waits for them, and re-layouts: 1.23 us -> 2.04 us
  transfers between devices with their start and end apart: 0 -> 1, of which waited for: 0 -> 0; matrix products, arithmetic and copies ran while one was open for 0% -> 3% of each run, Pallas kernels for 0% -> 54%
where the time goes in v3:
time: 87.4 us; the launch traced here: 86.2 us
  Pallas kernels  65.9 us (75%)
  between operations  14.8 us (17%)
  other arithmetic  2.46 us (3%)
  local copies, waits for them, and re-layouts  2.29 us (3%)
    pallas_call x1, Pallas kernels, spread_interp(): pl.pallas_call(functools.partial(spread_kernel, groups, vox, rows_dev, (G...  27.6 us
    pallas_call x1, Pallas kernels, solve(): pl.pallas_call(functools.partial(solve_kernel, (DELAYS * width) ** (-0.5)...  19.7 us
    pallas_call x1, Pallas kernels, gram_sum(): pl.pallas_call(functools.partial(gram_kernel, n, 1.0 / (DELAYS * width)),...  18.7 us
    unnamed x6, local copies, waits for them, and re-layouts  2.04 us
  transfers between devices with their start and end apart: 1, of which 0 were waited for; matrix products, arithmetic and copies ran while one was open for 3% of the time, Pallas kernels for 54%

profile of v3, /device:TPU:0, one launch (start us, length us, event | category | flops | bytes accessed | tf_op | source)
XLA Modules:
  0.0 86.2 jit_solution(9487698491051412494)
XLA Ops:
  6.5 0.0 all-gather.2.cloned.1.call-start
  6.5 0.7 all-gather.2.cloned.1.call-update
  8.6 0.8 fusion.1
  9.4 0.1 slice.27
  9.4 0.1 fusion.2
  9.5 0.1 pad_add_fusion
  9.6 0.0 copy-start.2
  9.6 1.2 %copy-done.2 = bf16[128,4096]{1,0:T(8,128)(2,1)S(1)} copy-done((bf16[128,4096]{1,0:T(8,128)(2,1)S(1)}, bf16[128,4096]{1,0:T(8,128)(2,1)}, u32[]{:S(2)}) %copy-start.2) | copy-done | bytes 1048600
  10.8 27.6 %spread_interp.1 = bf16[512,512]{1,0:T(8,128)(2,1)S(1)} custom-call(bf16[128,4096]{1,0:T(8,128)(2,1)S(1)} %copy-done.2, s32[8,256]{1,0:T(8,128)S(1)} %broadcast_in_dim.75.tick_ref, s32[8,256]{1,0:T(8,128)S(1)} %broadcast_in_dim.76.shift_ref), custom_call_target="tpu_custom_call" | custom-call | tf_op jit(solution)/shard_map/spread_interp/pallas_call | solution.py:199
  38.4 0.1 reshape.36
  38.5 0.8 select_reduce_fusion.1
  39.3 0.1 select_reduce_fusion
  39.4 0.3 pad_select_fusion.2
  39.7 0.3 pad_select_fusion
  39.9 0.2 pad_maximum_fusion.stacked_ref
  40.1 0.0 copy-start
  40.1 18.7 %gram_sum.1.kernel_ref = f32[384,384]{1,0:T(8,128)S(1)} custom-call(bf16[384,2048]{1,0:T(8,128)(2,1)S(1)} %pad_maximum_fusion.stacked_ref), custom_call_target="tpu_custom_call" | custom-call | tf_op jit(solution)/shard_map/gram_sum/pallas_call | solution.py:296
  58.8 0.0 copy-start.1
  58.8 0.8 copy-done.1
  59.6 0.0 all-gather.2.cloned.1.call-done.targets_ref
  59.6 0.0 copy-done
  59.6 19.7 %ridge_solve.1 = bf16[1,4,512,1024]{3,2,1,0:T(8,128)(2,1)} custom-call(f32[384,384]{1,0:T(8,128)} %copy-done.1, f32[1]{0:T(128)S(6)} %copy.8.penalty_ref, f32[8,384,128]{2,1,0:T(8,128)} %all-gather.2.cloned.1.call-done.targets_ref, bf16[384,2048]{1,0:T(8,128)(2,1)} %copy-done), custom_call_target="tpu_custom_call" | custom-call | tf_op jit(solution)/shard_map/ridge_solve/pallas_call | solution.py:439
  (5 shorter events, 0.0 us)
Async XLA Ops:
  6.5 53.1 %all-gather.2.cloned.1.call-start = ((), (), s32[]{:S(2)}) async-start(), calls=%async_computation | async-start | bytes 1769472 | tf_op jit(solution)/shard_map/all_gather | solution.py:469
  9.6 1.2 %copy-start.2 = (bf16[128,4096]{1,0:T(8,128)(2,1)S(1)}, bf16[128,4096]{1,0:T(8,128)(2,1)}, u32[]{:S(2)}) copy-start(bf16[128,4096]{1,0:T(8,128)(2,1)} %feat_ref.1) | copy-start | bytes 3145732
  40.1 19.5 %copy-start = (bf16[384,2048]{1,0:T(8,128)(2,1)}, bf16[384,2048]{1,0:T(8,128)(2,1)S(1)}, u32[]{:S(2)}) copy-start(bf16[384,2048]{1,0:T(8,128)(2,1)S(1)} %pad_maximum_fusion.stacked_ref) | copy-start | bytes 4718596
  58.8 0.8 copy-start.1
Sparse Core Ops, SparseCore 0:
  9.2 32.2 all-gather.1

commit v4 on v3

--- a/solution.py
+++ b/solution.py
@@ -35,8 +35,9 @@
     return jnp.where(x == 0, 1.0, jnp.sin(angle) / jnp.where(x == 0, 1.0, angle))
 
 
-def spread_kernel(groups, vox, rows_dev, scale, feat_ref, tick_ref, shift_ref, out_ref,
-                  edges, shifts, held, send_o, recv_o, send_e, recv_e, send_x, recv_x):
+def spread_kernel(groups, vox, rows_dev, scale, share, feat_ref, tick_ref, shift_ref, target_ref,
+                  out_ref, half_ref, edges, shifts, held, send_o, recv_o, send_e, recv_e,
+                  send_x, recv_x, send_r, recv_r):
     tok_dev, width = feat_ref.shape
     slab = width // vox
     halo = edges.shape[0] // 2
@@ -88,6 +89,25 @@
             device_id=place(peer), device_id_type=MESH,
         )
 
+    chips = vox // 2
+    chip, core = my_vox // 2, lax.rem(my_vox, 2)
+
+    def lend(turn):
+        other = lax.rem(chip + turn, chips)
+        return pltpu.make_async_remote_copy(
+            src_ref=target_ref, dst_ref=half_ref.at[chip],
+            send_sem=send_r.at[turn], recv_sem=recv_r.at[chip],
+            device_id={"vox": other * 2 + core}, device_id_type=MESH,
+        )
+
+    def lent(turn):
+        other = lax.rem(chip + turn, chips)
+        return pltpu.make_async_remote_copy(
+            src_ref=target_ref, dst_ref=half_ref.at[other],
+            send_sem=send_r.at[turn], recv_sem=recv_r.at[other],
+            device_id={"vox": other * 2 + core}, device_id_type=MESH,
+        )
+
     for turn in range(1, groups):
         tell(turn).start()
 
@@ -106,6 +126,11 @@
     @pl.when(me == devices - 1)
     def _():
         edges[halo:, :] = jnp.zeros((halo, width), edges.dtype)
+
+    if share:
+        for turn in range(1, chips):
+            lend(turn).start()
+        half_ref[chip] = target_ref[...]
 
     for turn in range(1, groups):
         told(turn).wait_recv()
@@ -179,6 +204,12 @@
         other = lax.rem(me + turn, devices)
         give(other // vox, lax.rem(other, vox)).wait_send()
 
+    if share:
+        for turn in range(1, chips):
+            lent(turn).wait_recv()
+        for turn in range(1, chips):
+            lend(turn).wait_send()
+
     for turn in range(1, groups):
         tell(turn).wait_send()
 
@@ -191,16 +222,21 @@
         downward(me - 1).wait_send()
 
 
-def spread_interp(features, ticks, shift, groups, vox, rows_dev, halo):
+def spread_interp(features, ticks, shift, targets, share, groups, vox, rows_dev, halo):
     tok_dev, width = features.shape
     devices = groups * vox
     slab = width // vox
     lanes = ticks.shape[1]
     return pl.pallas_call(
-        functools.partial(spread_kernel, groups, vox, rows_dev, (GAP / TICKS) ** 0.5),
-        out_shape=jax.ShapeDtypeStruct((devices * 16, slab), jnp.bfloat16),
-        in_specs=[pl.BlockSpec(memory_space=pltpu.VMEM)] * 3,
-        out_specs=pl.BlockSpec(memory_space=pltpu.VMEM),
+        functools.partial(
+            spread_kernel, groups, vox, rows_dev, (GAP / TICKS) ** 0.5, share
+        ),
+        out_shape=[
+            jax.ShapeDtypeStruct((devices * 16, slab), jnp.bfloat16),
+            jax.ShapeDtypeStruct((vox // 2, *targets.shape), jnp.float32),
+        ],
+        in_specs=[pl.BlockSpec(memory_space=pltpu.VMEM)] * 4,
+        out_specs=[pl.BlockSpec(memory_space=pltpu.VMEM)] * 2,
         scratch_shapes=[
             pltpu.VMEM((2 * halo, width), jnp.bfloat16),
             pltpu.VMEM((groups, 8, lanes), jnp.int32),
@@ -211,33 +247,54 @@
             pltpu.SemaphoreType.DMA((2,)),
             pltpu.SemaphoreType.DMA((devices,)),
             pltpu.SemaphoreType.DMA((devices,)),
+            pltpu.SemaphoreType.DMA((vox // 2,)),
+            pltpu.SemaphoreType.DMA((vox // 2,)),
         ],
         compiler_params=pltpu.CompilerParams(
             collective_id=1, has_side_effects=True, vmem_limit_bytes=32 * 2**20
         ),
         name="spread_interp",
-    )(features, ticks, shift)
-
-
-def gram_kernel(n, scale, stacked_ref, out_ref, part, land, send_a, recv_a, send_b, recv_b):
+    )(features, ticks, shift, targets)
+
+
+def gram_kernel(n, scale, share, stacked_ref, half_ref, out_ref, other_ref, part, land,
+                send_a, recv_a, send_b, recv_b, pair_sem):
     me = lax.axis_index("vox")
-    total = out_ref.shape[0]
-    rows = total // n
+    blocks = stacked_ref.shape[0] // BLOCK
+    rows = out_ref.shape[0] // n
     barrier = pltpu.get_barrier_semaphore()
     for step in range(1, n):
         pl.semaphore_signal(
             barrier, inc=1, device_id={"vox": lax.rem(me + step, n)}, device_id_type=MESH
         )
 
-    @pl.loop(0, total // BLOCK)
-    def _(block):
-        here = pl.ds(pl.multiple_of(block * BLOCK, BLOCK), BLOCK)
-        part[here, :] = lax.dot_general(
-            stacked_ref[here, :], stacked_ref[...], (((1,), (1,)), ((), ())),
+    def fill(i, j):
+        def tall(index):
+            start = index * BLOCK
+            return pl.ds(start if isinstance(start, int) else pl.multiple_of(start, BLOCK), BLOCK)
+
+        part[tall(i * (i + 1) // 2 + j), :] = lax.dot_general(
+            stacked_ref[tall(i), :], stacked_ref[tall(j), :], (((1,), (1,)), ((), ())),
             preferred_element_type=jnp.float32,
         )
 
+    if blocks <= 4:
+        for i in range(blocks):
+            for j in range(i + 1):
+                fill(i, j)
+    else:
+
+        @pl.loop(0, blocks)
+        def _(i):
+            @pl.loop(0, i + 1)
+            def _(j):
+                fill(i, j)
+
     pl.semaphore_wait(barrier, n - 1)
+    hand = pltpu.make_async_remote_copy(
+        src_ref=half_ref, dst_ref=other_ref, send_sem=pair_sem.at[0], recv_sem=pair_sem.at[1],
+        device_id={"vox": me + 1 - 2 * lax.rem(me, 2)}, device_id_type=MESH,
+    )
 
     def rows_of(owner):
         return pl.ds(pl.multiple_of(owner * rows, rows), rows)
@@ -283,34 +340,43 @@
     out_ref[rows_of(me), :] = total_rows * scale
     for step in range(1, n):
         spread(step).start()
+    if share:
+        hand.start()
     for step in range(1, n):
         spread_in(step).wait_recv()
+    if share:
+        hand.wait()
     for step in range(1, n):
         share(step).wait_send()
         spread(step).wait_send()
 
 
-def gram_sum(stacked, n, width):
-    total = stacked.shape[0]
-    rows = total // n
+def gram_sum(stacked, half, share, n, width):
+    blocks = stacked.shape[0] // BLOCK
+    tall = blocks * (blocks + 1) // 2 * BLOCK
+    block = pl.BlockSpec(memory_space=pltpu.VMEM)
     return pl.pallas_call(
-        functools.partial(gram_kernel, n, 1.0 / (DELAYS * width)),
-        out_shape=jax.ShapeDtypeStruct((total, total), jnp.float32),
-        in_specs=[pl.BlockSpec(memory_space=pltpu.VMEM)],
-        out_specs=pl.BlockSpec(memory_space=pltpu.VMEM),
+        functools.partial(gram_kernel, n, 1.0 / (DELAYS * width), share),
+        out_shape=[
+            jax.ShapeDtypeStruct((tall, BLOCK), jnp.float32),
+            jax.ShapeDtypeStruct(half.shape, jnp.float32),
+        ],
+        in_specs=[block, block],
+        out_specs=[block, block],
         scratch_shapes=[
-            pltpu.VMEM((total, total), jnp.float32),
-            pltpu.VMEM((n, rows, total), jnp.float32),
+            pltpu.VMEM((tall, BLOCK), jnp.float32),
+            pltpu.VMEM((n, tall // n, BLOCK), jnp.float32),
             pltpu.SemaphoreType.DMA((n,)),
             pltpu.SemaphoreType.DMA((n,)),
             pltpu.SemaphoreType.DMA((n,)),
             pltpu.SemaphoreType.DMA((n,)),
+            pltpu.SemaphoreType.DMA((2,)),
         ],
         compiler_params=pltpu.CompilerParams(
             collective_id=0, has_side_effects=True, vmem_limit_bytes=48 * 2**20
         ),
         name="gram_sum",
-    )(stacked)
+    )(stacked, half)
 
 
 def full_dot(a, b):
@@ -370,31 +436,44 @@
                 work[here, total:] -= full_dot(work[here, there], work[there, total:])
 
 
-def fetch_all(kernel_ref, targets_ref, work, fetched):
-    parts, total, voxels = targets_ref.shape
-    fetches = [pltpu.make_async_copy(kernel_ref, work.at[:, :total], fetched.at[parts])]
-    for part in range(parts):
-        columns = slice(total + part * voxels, total + (part + 1) * voxels)
-        fetches.append(
-            pltpu.make_async_copy(targets_ref.at[part], work.at[:, columns], fetched.at[part])
-        )
+def unfold(kernel_ref, work, total):
+    for i in range(total // BLOCK):
+        rows = slice(i * BLOCK, (i + 1) * BLOCK)
+        for j in range(i + 1):
+            columns = slice(j * BLOCK, (j + 1) * BLOCK)
+            start = (i * (i + 1) // 2 + j) * BLOCK
+            block = kernel_ref[start:start + BLOCK, :]
+            work[rows, columns] = block
+            if j < i:
+                work[columns, rows] = block.T
+
+
+def dual_kernel(kernel_ref, penalty_ref, targets_ref, out_ref, work, pair):
+    total = targets_ref.shape[0]
+    unfold(kernel_ref, work, total)
+    work[:, total:] = targets_ref[...]
+    ridge(work, pair, total, penalty_ref[0])
+    out_ref[...] = work[:, total:].astype(out_ref.dtype)
+
+
+def solve_kernel(scale, kernel_ref, penalty_ref, half_ref, other_ref, stacked_ref, out_ref,
+                 work, pair, dual, result, done, fetched):
+    chips, total, voxels = half_ref.shape
+    core = lax.rem(lax.axis_index("vox"), 2)
+    fetches = []
+    for chip in range(chips):
+        for source, side in ((half_ref, core), (other_ref, 1 - core)):
+            start = pl.multiple_of(total + (2 * chip + side) * voxels, BLOCK)
+            fetches.append(
+                pltpu.make_async_copy(
+                    source.at[chip], work.at[:, pl.ds(start, voxels)], fetched.at[len(fetches)]
+                )
+            )
     for fetch in fetches:
         fetch.start()
+    unfold(kernel_ref, work, total)
     for fetch in fetches:
         fetch.wait()
-
-
-def dual_kernel(kernel_ref, penalty_ref, targets_ref, out_ref, work, pair, fetched):
-    total = targets_ref.shape[1]
-    fetch_all(kernel_ref, targets_ref, work, fetched)
-    ridge(work, pair, total, penalty_ref[0])
-    out_ref[...] = work[:, total:].astype(out_ref.dtype)
-
-
-def solve_kernel(scale, kernel_ref, penalty_ref, targets_ref, stacked_ref, out_ref,
-                 work, pair, dual, result, done, fetched):
-    total = targets_ref.shape[1]
-    fetch_all(kernel_ref, targets_ref, work, fetched)
     ridge(work, pair, total, penalty_ref[0])
     dual[...] = work[:, total:].astype(dual.dtype)
     slab = result.shape[1]
@@ -415,31 +494,31 @@
 
 def solve_dual(kernel, penalty, targets):
     total, voxels = targets.shape
-    away = pl.BlockSpec(memory_space=pl.ANY)
+    block = pl.BlockSpec(memory_space=pltpu.VMEM)
     return pl.pallas_call(
         dual_kernel,
         out_shape=jax.ShapeDtypeStruct((total, voxels), jnp.bfloat16),
-        in_specs=[away, pl.BlockSpec(memory_space=pltpu.SMEM), away],
+        in_specs=[block, pl.BlockSpec(memory_space=pltpu.SMEM), block],
         out_specs=pl.BlockSpec(memory_space=pltpu.VMEM),
         scratch_shapes=[
             pltpu.VMEM((total, total + voxels), jnp.float32),
             pltpu.VMEM((2 * BLOCK, BLOCK), jnp.float32),
-            pltpu.SemaphoreType.DMA((2,)),
         ],
         compiler_params=pltpu.CompilerParams(vmem_limit_bytes=48 * 2**20),
         name="ridge_dual",
-    )(kernel, penalty, targets[None])
-
-
-def solve(kernel, penalty, targets, stacked, width):
-    parts, total, voxels = targets.shape
+    )(kernel, penalty, targets)
+
+
+def solve(kernel, penalty, half, other, stacked, width):
+    chips, total, voxels = half.shape
+    parts = 2 * chips
     slab = stacked.shape[1] // DELAYS
     block = pl.BlockSpec(memory_space=pltpu.VMEM)
     away = pl.BlockSpec(memory_space=pl.ANY)
     return pl.pallas_call(
         functools.partial(solve_kernel, (DELAYS * width) ** (-0.5)),
         out_shape=jax.ShapeDtypeStruct((1, DELAYS, slab, parts * voxels), jnp.bfloat16),
-        in_specs=[away, pl.BlockSpec(memory_space=pltpu.SMEM), away, block],
+        in_specs=[block, pl.BlockSpec(memory_space=pltpu.SMEM), away, away, block],
         out_specs=pl.BlockSpec(memory_space=pl.ANY),
         scratch_shapes=[
             pltpu.VMEM((total, total + parts * voxels), jnp.float32),
@@ -447,11 +526,11 @@
             pltpu.VMEM((total, parts * voxels), jnp.bfloat16),
             pltpu.VMEM((DELAYS, slab, parts * voxels), jnp.bfloat16),
             pltpu.SemaphoreType.DMA((DELAYS,)),
-            pltpu.SemaphoreType.DMA((parts + 1,)),
+            pltpu.SemaphoreType.DMA((parts,)),
         ],
         compiler_params=pltpu.CompilerParams(vmem_limit_bytes=60 * 2**20),
         name="ridge_solve",
-    )(kernel, penalty, targets, stacked)
+    )(kernel, penalty, half, other, stacked)
 
 
 def body(features, token_ticks, offsets, run_lengths, penalty, responses):
@@ -465,8 +544,7 @@
     halo = 3 * TICKS // GAP
     me = lax.axis_index("subj") * vox_count + lax.axis_index("vox")
     whole = tr_total <= 4 * BLOCK
-    if whole:
-        targets = lax.all_gather(responses[0], "vox", axis=0)
+    targets = responses[0] if whole else responses[0, :8]
 
     far = jnp.full((tok_dev,), -(2**20), jnp.int32)
     padded = jnp.concatenate([far, token_ticks, far])
@@ -476,13 +554,15 @@
     )
     ticks = jnp.broadcast_to(ticks, (8, 2 * tok_dev))
     shift = jnp.broadcast_to(offsets[0], (8, 2 * tok_dev))
-    blocks = spread_interp(features, ticks, shift, group_count, vox_count, rows_dev, halo)
+    blocks, half = spread_interp(
+        features, ticks, shift, targets, whole, group_count, vox_count, rows_dev, halo
+    )
     interp = blocks.reshape(devices, 16, slab_width)[:, :rows_dev].reshape(tr_total, slab_width)
 
     stacked = delay_stack(interp, run_lengths[0], tr_total)
-    kernel = gram_sum(stacked, vox_count, width)
+    kernel, other = gram_sum(stacked, half, whole, vox_count, width)
     if whole:
-        return solve(kernel, penalty, targets, stacked, width)
+        return solve(kernel, penalty, half, other, stacked, width)
     dual_coef = solve_dual(kernel, penalty, responses[0])
     projected = lax.dot_general(
         stacked,

time: 87.4 us -> 71.5 us (0.82)
  between operations: 14.8 us -> 1.39 us
  Pallas kernels: 65.9 us -> 62.5 us
  local copies, waits for them, and re-layouts: 2.29 us -> 4.06 us
    pallas_call x1, Pallas kernels: 18.7 us -> 13.4 us  [gram_sum(): pl.pallas_call(functools.partial(gram_kernel, n, 1.0 / (DELAYS * width),...]
    pallas_call x1, Pallas kernels: 27.6 us -> 30.3 us  [spread_interp(): pl.pallas_call(functools.partial(spread_kernel, groups, vox, rows_dev, (G...]
    unnamed x6 -> x12, local copies, waits for them, and re-layouts: 2.04 us -> 3.81 us
  transfers between devices with their start and end apart: 1 -> 0, of which waited for: 0 -> 0; matrix products, arithmetic and copies ran while one was open for 3% -> 0% of each run, Pallas kernels for 54% -> 0%
where the time goes in v4:
time: 71.5 us; the launch traced here: 70.5 us
  Pallas kernels  62.5 us (87%)
  local copies, waits for them, and re-layouts  4.06 us (6%)
  other arithmetic  2.46 us (3%)
  between operations  1.39 us (2%)
    pallas_call x1, Pallas kernels, spread_interp(): pl.pallas_call(functools.partial(spread_kernel, groups, vox, rows_dev, (G...  30.3 us
    pallas_call x1, Pallas kernels, solve(): pl.pallas_call(functools.partial(solve_kernel, (DELAYS * width) ** (-0.5)...  18.8 us
    pallas_call x1, Pallas kernels, gram_sum(): pl.pallas_call(functools.partial(gram_kernel, n, 1.0 / (DELAYS * width),...  13.4 us
    unnamed x12, local copies, waits for them, and re-layouts  3.81 us

profile of v4, /device:TPU:0, one launch (start us, length us, event | category | flops | bytes accessed | tf_op | source)
XLA Modules:
  0.0 70.5 jit_solution(5291724060593795363)
XLA Ops:
  1.3 0.8 %select_reduce_fusion.1 = s32[8]{0:T(128)S(1)} fusion(s32[8]{0:T(128)} %bitcast.16), kind=kLoop, calls=%fused_computation.10 | loop fusion | flops 184 | bytes 64 | tf_op jit(solution)/shard_map/reduce_sum | solution.py:20
  2.1 0.8 %fusion.1 = s32[192]{0:T(256)S(1)} fusion(s32[]{:T(128)S(6)} %select_n.26, s32[128]{0:T(128)S(1)} %broadcast_in_dim.74, s32[4096]{0:T(1024)} %param.7), kind=kLoop, calls=%fused_computation.17 | loop fusion | flops 384 | bytes 17668 | tf_op jit(solution)/shard_map/concatenate | solution.py:550
  2.9 0.1 slice.27
  2.9 0.1 fusion.2
  3.0 0.1 pad_add_fusion
  3.1 0.1 select_reduce_fusion
  3.2 0.0 copy-start.2
  3.2 1.2 %copy-done.2 = bf16[128,4096]{1,0:T(8,128)(2,1)S(1)} copy-done((bf16[128,4096]{1,0:T(8,128)(2,1)S(1)}, bf16[128,4096]{1,0:T(8,128)(2,1)}, u32[]{:S(2)}) %copy-start.2) | copy-done | bytes 1048600
  4.4 0.0 copy-start.5
  4.4 0.9 %copy-done.5 = f32[1,384,128]{2,1,0:T(8,128)S(1)} copy-done((f32[1,384,128]{2,1,0:T(8,128)S(1)}, f32[1,384,128]{2,1,0:T(8,128)}, u32[]{:S(2)}) %copy-start.5) | copy-done | bytes 196632
  5.4 30.3 %spread_interp.1 = (bf16[512,512]{1,0:T(8,128)(2,1)S(1)}, f32[4,384,128]{2,1,0:T(8,128)S(1)}) custom-call(bf16[128,4096]{1,0:T(8,128)(2,1)S(1)} %copy-done.2, s32[8,256]{1,0:T(8,128)S(1)} %broadcast_in_dim.75.tick_ref, s32[8,256]{1,0:T(8,128)S(1)} %broadcast_in_dim.76.shift_ref, f32[384,128]{1,0:T(8,128)S(1)} %bitcast.11), custom_call_target="tpu_custom_call" | custom-call | tf_op jit(solution)/shard_map/spread_interp/pallas_call | solution.py:230
  35.7 0.0 copy-start.1
  35.7 0.1 reshape.36
  35.8 0.3 pad_select_fusion.2
  36.1 0.3 pad_select_fusion
  36.4 0.2 pad_maximum_fusion.stacked_ref
  36.6 0.0 copy-done.1
  36.6 0.0 copy-start
  36.6 13.4 %gram_sum.1 = (f32[768,128]{1,0:T(8,128)S(1)}, f32[4,384,128]{2,1,0:T(8,128)S(1)}) custom-call(bf16[384,2048]{1,0:T(8,128)(2,1)S(1)} %pad_maximum_fusion.stacked_ref, f32[4,384,128]{2,1,0:T(8,128)S(1)} %get-tuple-element.10.half_ref), custom_call_target="tpu_custom_call" | custom-call | tf_op jit(solution)/shard_map/gram_sum/pallas_call | solution.py:358
  50.0 0.0 copy-start.3
  50.0 0.9 %copy-done.3 = f32[4,384,128]{2,1,0:T(8,128)} copy-done((f32[4,384,128]{2,1,0:T(8,128)}, f32[4,384,128]{2,1,0:T(8,128)S(1)}, u32[]{:S(2)}) %copy-start.3) | copy-done | bytes 786456
  50.9 0.0 copy-start.4
  50.9 0.7 %copy-done.4 = f32[768,128]{1,0:T(8,128)} copy-done((f32[768,128]{1,0:T(8,128)}, f32[768,128]{1,0:T(8,128)S(1)}, u32[]{:S(2)}) %copy-start.4) | copy-done | bytes 393240
  51.6 0.0 copy-done
  51.6 18.8 %ridge_solve.1 = bf16[1,4,512,1024]{3,2,1,0:T(8,128)(2,1)} custom-call(f32[768,128]{1,0:T(8,128)} %copy-done.4, f32[1]{0:T(128)S(6)} %copy.8.penalty_ref, f32[4,384,128]{2,1,0:T(8,128)} %copy-done.1, f32[4,384,128]{2,1,0:T(8,128)} %copy-done.3, bf16[384,2048]{1,0:T(8,128)(2,1)} %copy-done), custom_call_target="tpu_custom_call" | custom-call | tf_op jit(solution)/shard_map/ridge_solve/pallas_call | solution.py:518
  (5 shorter events, 0.0 us)
Async XLA Ops:
  3.2 1.2 %copy-start.2 = (bf16[128,4096]{1,0:T(8,128)(2,1)S(1)}, bf16[128,4096]{1,0:T(8,128)(2,1)}, u32[]{:S(2)}) copy-start(bf16[128,4096]{1,0:T(8,128)(2,1)} %feat_ref.1) | copy-start | bytes 3145732
  4.4 0.9 %copy-start.5 = (f32[1,384,128]{2,1,0:T(8,128)S(1)}, f32[1,384,128]{2,1,0:T(8,128)}, u32[]{:S(2)}) copy-start(f32[1,384,128]{2,1,0:T(8,128)} %param.11) | copy-start | bytes 589828
  35.7 0.9 %copy-start.1 = (f32[4,384,128]{2,1,0:T(8,128)}, f32[4,384,128]{2,1,0:T(8,128)S(1)}, u32[]{:S(2)}) copy-start(f32[4,384,128]{2,1,0:T(8,128)S(1)} %get-tuple-element.10.half_ref) | copy-start | bytes 2359300
  36.6 15.0 %copy-start = (bf16[384,2048]{1,0:T(8,128)(2,1)}, bf16[384,2048]{1,0:T(8,128)(2,1)S(1)}, u32[]{:S(2)}) copy-start(bf16[384,2048]{1,0:T(8,128)(2,1)S(1)} %pad_maximum_fusion.stacked_ref) | copy-start | bytes 4718596
  50.0 0.9 %copy-start.3 = (f32[4,384,128]{2,1,0:T(8,128)}, f32[4,384,128]{2,1,0:T(8,128)S(1)}, u32[]{:S(2)}) copy-start(f32[4,384,128]{2,1,0:T(8,128)S(1)} %get-tuple-element.12.other_ref) | copy-start | bytes 2359300
  50.9 0.7 %copy-start.4 = (f32[768,128]{1,0:T(8,128)}, f32[768,128]{1,0:T(8,128)S(1)}, u32[]{:S(2)}) copy-start(f32[768,128]{1,0:T(8,128)S(1)} %get-tuple-element.11.kernel_ref) | copy-start | bytes 1179652

commit v5 on v4

--- a/solution.py
+++ b/solution.py
@@ -35,9 +35,9 @@
     return jnp.where(x == 0, 1.0, jnp.sin(angle) / jnp.where(x == 0, 1.0, angle))
 
 
-def spread_kernel(groups, vox, rows_dev, scale, share, feat_ref, tick_ref, shift_ref, target_ref,
+def spread_kernel(groups, vox, rows_dev, scale, share, store_ref, tick_ref, shift_ref, target_ref,
                   out_ref, half_ref, edges, shifts, held, send_o, recv_o, send_e, recv_e,
-                  send_x, recv_x, send_r, recv_r):
+                  send_x, recv_x, send_r, recv_r, feat_ref, near_sem):
     tok_dev, width = feat_ref.shape
     slab = width // vox
     halo = edges.shape[0] // 2
@@ -57,6 +57,11 @@
             barrier, inc=1, device_id=place(lax.rem(me + turn, devices)), device_id_type=MESH
         )
 
+    fetch = pltpu.make_async_copy(store_ref, feat_ref, near_sem.at[0])
+    fetch.start()
+    keep = pltpu.make_async_copy(target_ref, half_ref.at[my_vox // 2], near_sem.at[1])
+    if share:
+        keep.start()
     shifts[my_group] = shift_ref[...]
     pl.semaphore_wait(barrier, devices - 1)
 
@@ -77,14 +82,14 @@
 
     def upward(peer):
         return pltpu.make_async_remote_copy(
-            src_ref=feat_ref.at[tok_dev - halo:, :], dst_ref=edges.at[:halo, :],
+            src_ref=store_ref.at[tok_dev - halo:, :], dst_ref=edges.at[:halo, :],
             send_sem=send_e.at[0], recv_sem=recv_e.at[0],
             device_id=place(peer), device_id_type=MESH,
         )
 
     def downward(peer):
         return pltpu.make_async_remote_copy(
-            src_ref=feat_ref.at[:halo, :], dst_ref=edges.at[halo:, :],
+            src_ref=store_ref.at[:halo, :], dst_ref=edges.at[halo:, :],
             send_sem=send_e.at[1], recv_sem=recv_e.at[1],
             device_id=place(peer), device_id_type=MESH,
         )
@@ -126,11 +131,6 @@
     @pl.when(me == devices - 1)
     def _():
         edges[halo:, :] = jnp.zeros((halo, width), edges.dtype)
-
-    if share:
-        for turn in range(1, chips):
-            lend(turn).start()
-        half_ref[chip] = target_ref[...]
 
     for turn in range(1, groups):
         told(turn).wait_recv()
@@ -144,6 +144,7 @@
         shaped = sinc(scaled) * sinc(scaled / 3.0)
         pieces.append(jnp.where(inside, shaped, jnp.zeros_like(shaped)))
     table = jnp.concatenate(pieces, axis=0).astype(jnp.bfloat16)
+    fetch.wait()
     inner = table[:, :tok_dev]
     outer = table[:, tok_dev:tok_dev + 2 * halo]
 
@@ -189,6 +190,10 @@
         for turn in range(groups):
             give(lax.rem(my_group + turn, groups), index).start()
 
+    if share:
+        for turn in range(1, chips):
+            lend(turn).start()
+
     make(my_vox)
     for turn in range(1, groups):
         give(lax.rem(my_group + turn, groups), my_vox).start()
@@ -205,6 +210,7 @@
         give(other // vox, lax.rem(other, vox)).wait_send()
 
     if share:
+        keep.wait()
         for turn in range(1, chips):
             lent(turn).wait_recv()
         for turn in range(1, chips):
@@ -227,6 +233,8 @@
     devices = groups * vox
     slab = width // vox
     lanes = ticks.shape[1]
+    block = pl.BlockSpec(memory_space=pltpu.VMEM)
+    far = pl.BlockSpec(memory_space=pltpu.HBM)
     return pl.pallas_call(
         functools.partial(
             spread_kernel, groups, vox, rows_dev, (GAP / TICKS) ** 0.5, share
@@ -235,8 +243,8 @@
             jax.ShapeDtypeStruct((devices * 16, slab), jnp.bfloat16),
             jax.ShapeDtypeStruct((vox // 2, *targets.shape), jnp.float32),
         ],
-        in_specs=[pl.BlockSpec(memory_space=pltpu.VMEM)] * 4,
-        out_specs=[pl.BlockSpec(memory_space=pltpu.VMEM)] * 2,
+        in_specs=[far, block, block, far],
+        out_specs=[block, far],
         scratch_shapes=[
             pltpu.VMEM((2 * halo, width), jnp.bfloat16),
             pltpu.VMEM((groups, 8, lanes), jnp.int32),
@@ -249,9 +257,11 @@
             pltpu.SemaphoreType.DMA((devices,)),
             pltpu.SemaphoreType.DMA((vox // 2,)),
             pltpu.SemaphoreType.DMA((vox // 2,)),
+            pltpu.VMEM((tok_dev, width), jnp.bfloat16),
+            pltpu.SemaphoreType.DMA((2,)),
         ],
         compiler_params=pltpu.CompilerParams(
-            collective_id=1, has_side_effects=True, vmem_limit_bytes=32 * 2**20
+            collective_id=1, has_side_effects=True, vmem_limit_bytes=61 * 2**20
         ),
         name="spread_interp",
     )(features, ticks, shift, targets)
@@ -355,14 +365,15 @@
     blocks = stacked.shape[0] // BLOCK
     tall = blocks * (blocks + 1) // 2 * BLOCK
     block = pl.BlockSpec(memory_space=pltpu.VMEM)
+    far = pl.BlockSpec(memory_space=pltpu.HBM)
     return pl.pallas_call(
         functools.partial(gram_kernel, n, 1.0 / (DELAYS * width), share),
         out_shape=[
             jax.ShapeDtypeStruct((tall, BLOCK), jnp.float32),
             jax.ShapeDtypeStruct(half.shape, jnp.float32),
         ],
-        in_specs=[block, block],
-        out_specs=[block, block],
+        in_specs=[block, far],
+        out_specs=[block, far],
         scratch_shapes=[
             pltpu.VMEM((tall, BLOCK), jnp.float32),
             pltpu.VMEM((n, tall // n, BLOCK), jnp.float32),
@@ -515,10 +526,11 @@
     slab = stacked.shape[1] // DELAYS
     block = pl.BlockSpec(memory_space=pltpu.VMEM)
     away = pl.BlockSpec(memory_space=pl.ANY)
+    far = pl.BlockSpec(memory_space=pltpu.HBM)
     return pl.pallas_call(
         functools.partial(solve_kernel, (DELAYS * width) ** (-0.5)),
         out_shape=jax.ShapeDtypeStruct((1, DELAYS, slab, parts * voxels), jnp.bfloat16),
-        in_specs=[block, pl.BlockSpec(memory_space=pltpu.SMEM), away, away, block],
+        in_specs=[block, pl.BlockSpec(memory_space=pltpu.SMEM), far, far, block],
         out_specs=pl.BlockSpec(memory_space=pl.ANY),
         scratch_shapes=[
             pltpu.VMEM((total, total + parts * voxels), jnp.float32),
@@ -528,7 +540,7 @@
             pltpu.SemaphoreType.DMA((DELAYS,)),
             pltpu.SemaphoreType.DMA((parts,)),
         ],
-        compiler_params=pltpu.CompilerParams(vmem_limit_bytes=60 * 2**20),
+        compiler_params=pltpu.CompilerParams(vmem_limit_bytes=24 * 2**20),
         name="ridge_solve",
     )(kernel, penalty, half, other, stacked)
 

time: 71.5 us -> 70.3 us (0.983)
  local copies, waits for them, and re-layouts: 4.06 us -> 2.83 us
    unnamed x12 -> x2, local copies, waits for them, and re-layouts: 3.81 us -> 0.36 us
    pallas_call x1, Pallas kernels: 18.8 us -> 15.8 us  [solve(): pl.pallas_call(functools.partial(solve_kernel, (DELAYS * width) ** (-0.5)...]
    pallas_call x1, Pallas kernels: 30.3 us -> 33.2 us  [spread_interp(): pl.pallas_call(functools.partial(spread_kernel, groups, vox, rows_dev, (G...]
    reshape x1, local copies, waits for them, and re-layouts: 0.09 us -> 1.13 us  [body(): blocks.reshape(devices, 16, slab_width)[:, :rows_dev]]
where the time goes in v5:
time: 70.3 us; the launch traced here: 69.5 us
  Pallas kernels  62.8 us (89%)
  local copies, waits for them, and re-layouts  2.83 us (4%)
  other arithmetic  2.48 us (4%)
  between operations  1.35 us (2%)
    pallas_call x1, Pallas kernels, spread_interp(): pl.pallas_call(functools.partial(spread_kernel, groups, vox, rows_dev, (G...  33.2 us
    pallas_call x1, Pallas kernels, solve(): pl.pallas_call(functools.partial(solve_kernel, (DELAYS * width) ** (-0.5)...  15.8 us
    pallas_call x1, Pallas kernels, gram_sum(): pl.pallas_call(functools.partial(gram_kernel, n, 1.0 / (DELAYS * width),...  13.8 us

profile of v5, /device:TPU:0, one launch (start us, length us, event | category | flops | bytes accessed | tf_op | source)
XLA Modules:
  0.0 69.5 jit_solution(14666412412303081998)
XLA Ops:
  1.3 0.8 %select_reduce_fusion.1 = s32[8]{0:T(128)S(1)} fusion(s32[8]{0:T(128)} %bitcast.16), kind=kLoop, calls=%fused_computation.10 | loop fusion | flops 184 | bytes 64 | tf_op jit(solution)/shard_map/reduce_sum | solution.py:20
  2.1 0.8 %fusion.1 = s32[192]{0:T(256)S(1)} fusion(s32[]{:T(128)S(6)} %select_n.26, s32[128]{0:T(128)S(1)} %broadcast_in_dim.74, s32[4096]{0:T(1024)} %param.7), kind=kLoop, calls=%fused_computation.17 | loop fusion | flops 384 | bytes 17668 | tf_op jit(solution)/shard_map/concatenate | solution.py:562
  2.9 0.1 slice.27
  2.9 0.1 fusion.2
  3.0 0.1 pad_add_fusion
  3.1 0.1 select_reduce_fusion
  3.2 0.6 broadcast_in_dim.75.tick_ref
  3.8 0.6 broadcast_in_dim.76.shift_ref
  4.4 33.2 %spread_interp.1 = (bf16[512,512]{1,0:T(8,128)(2,1)}, f32[4,384,128]{2,1,0:T(8,128)}) custom-call(bf16[128,4096]{1,0:T(8,128)(2,1)} %store_ref.1, s32[8,256]{1,0:T(8,128)} %broadcast_in_dim.75.tick_ref, s32[8,256]{1,0:T(8,128)} %broadcast_in_dim.76.shift_ref, f32[384,128]{1,0:T(8,128)} %bitcast.15), custom_call_target="tpu_custom_call" | custom-call | tf_op jit(solution)/shard_map/spread_interp/pallas_call | solution.py:238
  37.6 1.1 %reshape.36 = bf16[384,512]{1,0:T(8,128)(2,1)S(1)} reshape(bf16[32,12,512]{2,1,0:T(8,128)(2,1)} %bitcast.14) | data formatting | bytes 786432 | tf_op jit(solution)/shard_map/reshape | solution.py:572
  38.7 0.0 copy-start
  38.8 0.3 pad_select_fusion.2
  39.0 0.3 pad_select_fusion
  39.3 0.2 pad_maximum_fusion.stacked_ref
  39.5 0.4 copy-done
  39.9 13.8 %gram_sum.1 = (f32[768,128]{1,0:T(8,128)S(1)}, f32[4,384,128]{2,1,0:T(8,128)S(1)}) custom-call(bf16[384,2048]{1,0:T(8,128)(2,1)S(1)} %pad_maximum_fusion.stacked_ref, f32[4,384,128]{2,1,0:T(8,128)S(1)} %copy-done), custom_call_target="tpu_custom_call" | custom-call | tf_op jit(solution)/shard_map/gram_sum/pallas_call | solution.py:369
  53.7 15.8 %ridge_solve.1 = bf16[1,4,512,1024]{3,2,1,0:T(8,128)(2,1)} custom-call(f32[768,128]{1,0:T(8,128)S(1)} %get-tuple-element.11.kernel_ref, f32[1]{0:T(128)S(6)} %copy.8.penalty_ref, f32[4,384,128]{2,1,0:T(8,128)S(1)} %copy-done, f32[4,384,128]{2,1,0:T(8,128)S(1)} %get-tuple-element.12.other_ref, bf16[384,2048]{1,0:T(8,128)(2,1)S(1)} %pad_maximum_fusion.stacked_ref), custom_call_target="tpu_custom_call" | custom-call | tf_op jit(solution)/shard_map/ridge_solve/pallas_call | solution.py:530
  (3 shorter events, 0.0 us)
Async XLA Ops:
  38.7 1.1 %copy-start = (f32[4,384,128]{2,1,0:T(8,128)S(1)}, f32[4,384,128]{2,1,0:T(8,128)}, u32[]{:S(2)}) copy-start(f32[4,384,128]{2,1,0:T(8,128)} %get-tuple-element.10.half_ref) | copy-start | bytes 2359300
